TPU v7x, 256 devices: a whole 4x4x8 slice. The times are simulated.
256 devices in a mesh: cache: 32 (over y, x, core), tp: 8 (over z).
Axes of the slice: x: 4, y: 4, z: 8, core: 2. Of those that a mesh axis runs over, the one named last changes fastest.
Arguments:
- tokens: bfloat16 [16384, 4096], P(('cache', 'tp')), may hold values from -6 to 6
- weight_x: bfloat16 [4096, 8192], P(None, 'tp'), may hold values from -0.09375 to 0.09375
- weight_bc: bfloat16 [4096, 2, 1024], P(None, None, 'tp'), may hold values from -0.046875 to 0.046875
- weight_dt: bfloat16 [4096, 128], P(None, 'tp'), may hold values from -0.09375 to 0.09375
- kernel_x: bfloat16 [4, 8192], P(None, 'tp'), may hold values from -3 to 3
- kernel_bc: bfloat16 [4, 2, 1024], P(None, None, 'tp'), may hold values from -3 to 3
- dt_bias: float32 [128], P('tp'), may hold values from -3 to -1
- decay_rate: float32 [128], P('tp'), may hold values from 0.05 to 8
- skip_gain: float32 [128], P('tp'), may hold values from 0.5 to 1.5
- ssm_pool: bfloat16 [64, 128, 64, 128], P('cache', 'tp'), may hold values from -2 to 2
- conv_x_pool: bfloat16 [64, 3, 8192], P('cache', None, 'tp'), may hold values from -6 to 6
- conv_bc_pool: bfloat16 [64, 3, 2, 1024], P('cache', None, None, 'tp'), may hold values from -3 to 3
- hit_holder: int32 [1024, 1], replicated, may hold values from 0 to 31; in each aligned block of 32 rows (0 to 31, 32 to 63, ...) at most 2 rows name the same one
- hit_slot: int32 [1024], replicated, may hold values from 0 to 1
- suffix_len: int32 [32, 32], P('cache'), may hold values from 1 to 32, 512 in all within a row
Outputs:
- mixed: bfloat16 [16384, 8192], P('cache', 'tp')
Inputs may be any that keep to these rules, and one draw needn't show every extreme that they name: `hit_holder`: row o * 32 + k is request k of group o; among the 32 requests of one group at most 2 name the same holder, and some group reaches 2. `suffix_len`: the 32 lengths of one group sum to 512; the longest of all is exactly 32.
All inputs are finite; a program needn't handle non-finite values.
Results may differ from a plain program's by a relative error of at most 0.014.
Values may be sent and summed in bfloat16 or wider, within the bound.
No kernel may reach another device: no remote copies, remote signals or barrier semaphores. Data moves between devices by JAX's collectives and lax.ppermute only.
A program may use at most 128 MiB of HBM per device.

v0:
```python
import jax
import jax.numpy as jnp
from jax import lax
from jax.experimental import pallas as pl
from jax.experimental.pallas import tpu as pltpu
from jax.sharding import PartitionSpec as P

NX, NY, NZ = 4, 4, 8
MOST = 60 * 1024 * 1024
TILE = 64
PRIOR = 16
PRIORS = NX * PRIOR
WIDE = 512
F32, BF16 = jnp.float32, jnp.bfloat16


def chip(y, x, c):
    return (y % NY) * 2 * NX + (x % NX) * 2 + c


def every():
    return [(y, x, c) for y in range(NY) for x in range(NX) for c in range(2)]


def first_round(step):
    return [(chip(y, x, c), chip(y + c * step, x + (1 - c) * step, c)) for y, x, c in every()]


def second_round(step):
    return [(chip(y, x, c), chip(y + (1 - c) * step, x + c * step, c)) for y, x, c in every()]


CORES = [(chip(y, x, c), chip(y, x, 1 - c)) for y, x, c in every()]


def over_z(value, step):
    return lax.ppermute(value, "tp", [(z, (z + step) % NZ) for z in range(NZ)])


def on_cache(value, pairs):
    return lax.ppermute(value, "cache", pairs)


def moved(name, sources, shapes, moves):
    def kernel(*refs):
        ins, (outs, held, sems) = refs[: len(sources)], (refs[len(sources) : -2], refs[-2], refs[-1])
        inward, outward, first = [], [], 0
        for k, (src, at, count, dst, to) in enumerate(moves):
            spot = held.at[pl.ds(first, count), :]
            inward.append(pltpu.make_async_copy(ins[src].at[pl.ds(at, count), :], spot, sems.at[2 * k]))
            outward.append(pltpu.make_async_copy(spot, outs[dst].at[pl.ds(to, count), :], sems.at[2 * k + 1]))
            first += count
        for copy in inward:
            copy.start()
        for before, after in zip(inward, outward):
            before.wait()
            after.start()
        for copy in outward:
            copy.wait()

    rows = sum(move[2] for move in moves)
    return pl.pallas_call(
        kernel,
        out_shape=[jax.ShapeDtypeStruct(shape, sources[0].dtype) for shape in shapes],
        in_specs=[pl.BlockSpec(memory_space=pltpu.HBM)] * len(sources),
        out_specs=[pl.BlockSpec(memory_space=pltpu.HBM)] * len(shapes),
        scratch_shapes=[
            pltpu.VMEM((rows, sources[0].shape[1]), sources[0].dtype),
            pltpu.SemaphoreType.DMA((2 * len(moves),)),
        ],
        compiler_params=pltpu.CompilerParams(vmem_limit_bytes=MOST),
        cost_estimate=pl.CostEstimate(flops=0, bytes_accessed=4000000, transcendentals=0),
        name=name,
    )(*sources)


def lined(nodes):
    states, cols = nodes[0].shape[0] - PRIOR, nodes[0].shape[1]
    moves = []
    for k in range(len(nodes)):
        moves.append((k, 0, states, 0, k * states))
        moves.append((k, states, PRIOR, 1, k * PRIOR))
    return moved("lined", nodes, [(len(nodes) * states, cols), (len(nodes) * PRIOR, cols)], moves)


def stacked(parts):
    rows, cols = parts[0].shape
    moves = [(k, 0, rows, 0, k * rows) for k in range(len(parts))]
    return moved("stacked", parts, [(len(parts) * rows, cols)], moves)[0]


def halves(top, bottom):
    rows, cols = top.shape[0] // 2, top.shape[1]
    return moved("halves", [top, bottom], [(rows, cols)] * 2, [(0, 0, rows, 0, 0), (1, rows, rows, 1, 0)])


def gather(pool, tokens, tables, project, inner):
    tie = lax.optimization_barrier
    near_up, near_down = on_cache(pool, first_round(1)), on_cache(pool, first_round(-1))
    far = on_cache(pool, first_round(2))
    up, down = over_z(tokens, 1), over_z(tokens, -1)
    near_up, near_down, far, up, down, tables = tie((near_up, near_down, far, up, down, tables))

    blocks = [tokens, up, down]
    up, down = over_z(up, 1), over_z(down, -1)
    blocks += [up, down]
    line, line_prior = lined([pool, near_up, near_down, far])
    priors = [line_prior] + [on_cache(line_prior, second_round(step)) for step in (1, -1, 2)]
    line, priors = tie((line, priors))
    near_up, near_down = on_cache(line, second_round(1)), on_cache(line, second_round(-1))
    priors = stacked(priors)
    priors = [priors, on_cache(priors, CORES)]
    line_other = on_cache(line, CORES)
    blocks, line_other, priors = tie((blocks, line_other, priors))
    projected = project(blocks, tables[1])
    up, down = over_z(up, 1), over_z(down, -1)
    blocks = [up, down]
    near_up, near_down, up, down, projected = tie((near_up, near_down, up, down, projected))

    last_up, last_down = halves(up, down)
    blocks += [over_z(last_up, 1), over_z(last_down, -1)]
    far_up, far_down = halves(near_up, near_down)
    far_up, far_down = on_cache(far_up, second_round(1)), on_cache(far_down, second_round(-1))
    up_other, down_other, blocks = tie((near_up, near_down, blocks))
    up_other, down_other = on_cache(up_other, CORES), on_cache(down_other, CORES)
    result = inner(blocks, projected, [line, line_other, near_up, near_down], priors, tables)
    far_up, far_down, result = tie((far_up, far_down, result))
    far_others = [on_cache(far_up, CORES), on_cache(far_down, CORES)]
    return [up_other, down_other, far_up, far_others[0], far_down, far_others[1]], result


def dot(a, b):
    return jnp.dot(a, b, preferred_element_type=F32)


def dot_t(a, b):
    return lax.dot_general(a, b, (((1,), (1,)), ((), ())), preferred_element_type=F32)


def fetched(blocks, weights, tok, held, sem):
    w_x_in, w_bc_in, w_dt_in = weights
    w_x, w_bc, w_dt = held
    now, at = [], 0
    for block in blocks:
        now.append(pltpu.make_async_copy(block, tok.at[pl.ds(at, block.shape[0]), :], sem.at[len(now)]))
        at += block.shape[0]
    heads = w_dt_in.shape[0]
    now.append(pltpu.make_async_copy(w_bc_in, w_bc, sem.at[len(now)]))
    now.append(pltpu.make_async_copy(w_dt_in, w_dt.at[pl.ds(0, heads), :], sem.at[len(now)]))
    chunks = []
    for k in range(w_x.shape[1] // WIDE):
        here = (slice(None), slice(WIDE * k, WIDE * (k + 1)))
        chunks.append(pltpu.make_async_copy(w_x_in.at[here], w_x.at[here], sem.at[len(now) + k]))
    for copy in now + chunks:
        copy.start()
    w_dt[heads:, :] = jnp.zeros((128 - heads, w_dt.shape[1]), BF16)
    return now, chunks


def project_kernel(*refs):
    blocks, (w_x_in, w_bc_in, w_dt_in, x_out, b_out, tok, w_x, w_bc, w_dt, sem) = refs[:-10], refs[-10:]
    now, chunks = fetched(blocks, (w_x_in, w_bc_in, w_dt_in), tok, (w_x, w_bc, w_dt), sem)
    for copy in now:
        copy.wait()
    b_out[:, 0:256] = dot(tok[...], w_bc[...]).astype(BF16)
    b_out[:, 256:384] = dot_t(tok[...], w_dt[...]).astype(BF16)
    for k, copy in enumerate(chunks):
        copy.wait()
        here = slice(WIDE * k, WIDE * (k + 1))
        x_out[:, here] = dot(tok[...], w_x[:, here]).astype(BF16)


def inner_kernel(
    where, table, b0, b1, b2, b3, w_x_in, w_bc_in, w_dt_in, s0, s1, s2, s3, p0, p1,
    x_first, b_first, info, cols_in, taps, bias, decay, skip, sum_ref, c_ref, fade_ref,
    raw, xs, bs, cs, run, step, tok, w_x, w_bc, w_dt, sem, states, state_sem, prior, prior_sem,
):
    rows = raw.shape[0] - 8
    x_cols = w_x.shape[1]
    cols = taps.shape[1]
    block = rows // NZ
    z = where[0]
    now, chunks = fetched([b0, b1, b2, b3], (w_x_in, w_bc_in, w_dt_in), tok, (w_x, w_bc, w_dt), sem)
    parts = (s0, s1, s2, s3)
    fetch_states(table, 0, parts, states, state_sem)
    for k, source in enumerate((p0, p1)):
        spot = prior.at[pl.ds(k * p0.shape[0], p0.shape[0]), :]
        now.append(pltpu.make_async_copy(source, spot, prior_sem.at[k]))
        now[-1].start()

    def put(target, lead, columns, values, shifts):
        for k, shift in enumerate(shifts):
            at = pl.multiple_of(lax.rem(z + shift + NZ, NZ) * block, block)
            target[pl.ds(lead + at, block), columns] = values[k * block : (k + 1) * block].astype(F32)

    put(raw, 8, slice(0, x_cols), x_first, (0, -1, 1, -2, 2))
    put(raw, 8, slice(x_cols, cols), b_first[:, 0:256], (0, -1, 1, -2, 2))
    put(step, TILE, slice(None), b_first[:, 256:384], (0, -1, 1, -2, 2))
    raw[0:8, :] = jnp.zeros((8, cols), F32)

    position = lax.broadcasted_iota(jnp.int32, (rows, 128), 0)
    request = lax.broadcasted_iota(jnp.int32, (rows, 128), 1).astype(F32)
    req_col = jnp.sum(jnp.where(position >= info[0:1, :], 1.0, 0.0), axis=1, keepdims=True)
    is_own = request == req_col
    own_start = jnp.sum(jnp.where(is_own, info[1:2, :].astype(F32), 0.0), axis=1, keepdims=True)
    offset = position[:, 0:1].astype(F32) - own_start

    def requests_at(first, count):
        spot = first + lax.broadcasted_iota(jnp.int32, (info.shape[1], count), 1)
        found = jnp.sum(jnp.where(spot >= cols_in[:, 1:2], 1.0, 0.0), axis=0, keepdims=True)
        return jnp.where(spot[0:1] < 0, -1.0, found)

    before = lax.broadcasted_iota(jnp.int32, (rows, rows), 0) >= lax.broadcasted_iota(
        jnp.int32, (rows, rows), 1
    )
    sums = jnp.where((req_col == requests_at(0, rows)) & before, 1.0, 0.0).astype(BF16)
    slot_ids = lax.broadcasted_iota(jnp.int32, (cols_in.shape[0], prior.shape[0]), 1)
    pick_x = jnp.where(slot_ids == cols_in[:, 0:1], 1.0, 0.0).astype(BF16)
    pick_bc = jnp.where(slot_ids == cols_in[:, 0:1] + 6, 1.0, 0.0).astype(BF16)
    spot_ids = lax.broadcasted_iota(jnp.int32, (rows, cols_in.shape[0]), 1).astype(F32)
    chosen = [
        jnp.where((spot_ids == 3 * req_col + offset + (3 - lag)) & (offset < lag), 1.0, 0.0).astype(BF16)
        for lag in (1, 2, 3)
    ]
    xs[0:TILE, :] = jnp.zeros((TILE, x_cols), BF16)
    bs[0:TILE, :] = jnp.zeros((TILE, 128), BF16)
    run[0:TILE, :] = jnp.zeros((TILE, 128), F32)
    step[0:TILE, :] = jnp.zeros((TILE, 128), F32)
    c_ref[rows:, :] = jnp.zeros((c_ref.shape[0] - rows, 128), F32)

    def convolved(here, inputs):
        total = taps[3:4, here] * raw[8:, here]
        for lag in (1, 2, 3):
            shifted = raw[8 - lag : 8 - lag + rows, here]
            value = jnp.where(offset < lag, 0.0, shifted) + dot(chosen[lag - 1], inputs)
            total = total + taps[3 - lag : 4 - lag, here] * value
        return (total / (1.0 + jnp.exp(-total))).astype(BF16)

    for copy in now:
        copy.wait()
    put(raw, 8, slice(x_cols, cols), dot(tok[...], w_bc[...]).astype(BF16), (-3, 3, 4))
    put(step, TILE, slice(None), dot_t(tok[...], w_dt[...]).astype(BF16), (-3, 3, 4))
    out = convolved(slice(x_cols, cols), dot(pick_bc, prior[:, 0 : cols - x_cols]).astype(BF16))
    inputs = dot(pick_x, prior[...]).astype(BF16)
    bs[TILE:, :] = out[:, 0:128]
    cs[...] = out[:, 128:256]
    c_ref[0:rows, :] = out[:, 128:256].astype(F32)
    steps = jax.nn.softplus(step[TILE:, :] + bias[...])
    step[TILE:, :] = steps
    log_keep = -steps * decay[...]
    high = log_keep.astype(BF16)
    left = log_keep - high.astype(F32)
    middle = left.astype(BF16)
    low = (left - middle.astype(F32)).astype(BF16)
    running = dot(sums, high) + dot(sums, middle) + dot(sums, low)
    run[TILE:, :] = running
    fade_ref[0:rows, :] = jnp.exp(running)

    for k, copy in enumerate(chunks):
        copy.wait()
        here = slice(WIDE * k, WIDE * (k + 1))
        put(raw, 8, here, dot(tok[...], w_x[:, here]).astype(BF16), (-3, 3, 4))
        for at in range(WIDE * k, WIDE * (k + 1), 256):
            xs[TILE:, at : at + 256] = convolved(slice(at, at + 256), inputs[:, at : at + 256])

    lanes = lax.broadcasted_iota(jnp.int32, (TILE, 2 * TILE), 1)
    subs = lax.broadcasted_iota(jnp.int32, (TILE, 2 * TILE), 0)
    left = lax.broadcasted_iota(jnp.int32, (2 * TILE, 128), 1) < 64

    def tile(j, carry):
        at = pl.multiple_of(j * TILE, TILE)
        score = dot_t(cs[pl.ds(at, TILE), :], bs[pl.ds(at, 2 * TILE), :])
        around = requests_at(at - TILE, 2 * TILE)
        own = around.reshape(1, 2 * TILE)
        own_col = jnp.sum(
            jnp.where(at + subs >= info[0:1, :], 1.0, 0.0), axis=1, keepdims=True
        )
        mask = (own_col == own) & (lanes - TILE <= subs)
        run_w = run[pl.ds(at, 2 * TILE), :]
        run_rows = run_w.T
        step_rows = step[pl.ds(at, 2 * TILE), :].T
        run_cols = run_w[TILE:, :]
        for pair in range(x_cols // 128):
            mixes = []
            for h in (2 * pair, 2 * pair + 1):
                gap = run_cols[:, h : h + 1] - run_rows[h : h + 1, :]
                mix = jnp.exp(jnp.where(mask, gap, -jnp.inf)) * score * step_rows[h : h + 1, :]
                mixes.append(mix.astype(BF16))
            here = slice(128 * pair, 128 * (pair + 1))
            x_w = xs[pl.ds(at, 2 * TILE), here]
            nothing = jnp.zeros_like(x_w)
            both = jnp.concatenate([jnp.where(left, x_w, nothing), jnp.where(left, nothing, x_w)], axis=0)
            out = dot(jnp.concatenate(mixes, axis=1), both)
            sum_ref[pair, pl.ds(at, TILE), :] = out + skip[:, here] * x_w[TILE:].astype(F32)
        return carry

    lax.fori_loop(0, rows // TILE, tile, 0)
    sum_ref[:, rows:, :] = jnp.zeros((x_cols // 128, sum_ref.shape[1] - rows, 128), F32)
    fade_ref[rows:, :] = jnp.zeros((fade_ref.shape[0] - rows, 128), F32)
    add_carried(table, 0, parts, c_ref, fade_ref, states, sum_ref, state_sem)


def fetch_states(table, first, arrays, states, sems):
    state_size = states.shape[1]
    for k, array in enumerate(arrays):

        def begin(i, carry, array=array):
            at = pl.multiple_of(table[2, i] * state_size, state_size)
            pltpu.make_async_copy(array.at[pl.ds(at, state_size), :], states.at[i], sems.at[i]).start()
            return carry

        lax.fori_loop(table[3, first + k], table[3, first + k + 1], begin, 0)


def add_carried(table, first, arrays, c_ref, fade_ref, states, total, sems):
    requests, state_size, x_cols = states.shape
    begins, ends = table[3, first], table[3, first + len(arrays)]
    row = lax.broadcasted_iota(jnp.int32, (32, 128), 0)
    lane_head = lax.broadcasted_iota(jnp.int32, (128, x_cols), 1) // 64
    spread = jnp.where(lane_head == lax.broadcasted_iota(jnp.int32, (128, x_cols), 0), 1.0, 0.0).astype(BF16)
    side = 4

    def some(group, carry):
        picks = []
        for k in range(side):
            i = begins + group * side + k

            @pl.when(i < ends)
            def _():
                pltpu.make_async_copy(
                    arrays[0].at[pl.ds(0, state_size), :], states.at[i], sems.at[i]
                ).wait()

            safe = jnp.minimum(i, requests - 1)
            picks.append((safe, table[0, safe], jnp.where(i < ends, table[1, safe], 0)))
        terms = []
        for i, start, _ in picks:
            fade = fade_ref[pl.ds(start, 32), :]
            high = fade.astype(BF16)
            low = (fade - high.astype(F32)).astype(BF16)
            scale = dot(jnp.concatenate([high, low], axis=0), spread)
            product = dot(c_ref[pl.ds(start, 32), :].astype(BF16), states[i])
            terms.append((scale[0:32] + scale[32:64]) * product)
        for term, (_, start, length) in zip(terms, picks):
            inside = row < length
            for k in range(x_cols // 128):
                old = total[k, pl.ds(start, 32), :]
                total[k, pl.ds(start, 32), :] = jnp.where(
                    inside, old + term[:, 128 * k : 128 * (k + 1)], old
                )
        return carry

    lax.fori_loop(0, lax.div(ends - begins + side - 1, side), some, 0)


def late_kernel(first, count, table, *refs):
    arrays, (c_ref, fade_ref, before, out, states, total, sems, got) = refs[:count], refs[count:]
    rows = out.shape[0]
    copy = pltpu.make_async_copy(before, total, got)
    copy.start()
    fetch_states(table, first, arrays, states, sems)
    copy.wait()
    add_carried(table, first, arrays, c_ref, fade_ref, states, total, sems)
    for k in range(total.shape[0]):
        out[:, 128 * k : 128 * (k + 1)] = total[k, 0:rows, :].astype(BF16)


VMEM = pl.BlockSpec(memory_space=pltpu.VMEM)
SMEM = pl.BlockSpec(memory_space=pltpu.SMEM)
HBM = pl.BlockSpec(memory_space=pltpu.HBM)


def weight_scratch(weights, rows, copies):
    depth, x_cols = weights[0].shape
    return [
        pltpu.VMEM((rows, depth), BF16),
        pltpu.VMEM((depth, x_cols), BF16),
        pltpu.VMEM((depth, weights[1].shape[1]), BF16),
        pltpu.VMEM((128, depth), BF16),
        pltpu.SemaphoreType.DMA((copies + 2 + x_cols // WIDE,)),
    ]


def project(blocks, weights):
    rows, x_cols = sum(b.shape[0] for b in blocks), weights[0].shape[1]
    return pl.pallas_call(
        project_kernel,
        out_shape=(
            jax.ShapeDtypeStruct((rows, x_cols), BF16),
            jax.ShapeDtypeStruct((rows, weights[1].shape[1] + 128), BF16),
        ),
        in_specs=[HBM] * (len(blocks) + 3),
        out_specs=(VMEM, VMEM),
        scratch_shapes=weight_scratch(weights, rows, len(blocks)),
        compiler_params=pltpu.CompilerParams(vmem_limit_bytes=MOST),
        cost_estimate=pl.CostEstimate(flops=8000000000, bytes_accessed=14000000, transcendentals=0),
        name="project",
    )(*blocks, *weights)


def mixer_inner(z, table, blocks, weights, parts, priors, projected, info, columns, taps, bias, decay, skip):
    block_rows = blocks[0].shape[0]
    rows, x_cols, cols = NZ * block_rows, weights[0].shape[1], taps.shape[1]
    requests, state_size, margin = table.shape[1] - 1, 128, 32
    return pl.pallas_call(
        inner_kernel,
        out_shape=(
            jax.ShapeDtypeStruct((x_cols // 128, rows + margin, 128), F32),
            jax.ShapeDtypeStruct((rows + margin, 128), F32),
            jax.ShapeDtypeStruct((rows + margin, 128), F32),
        ),
        in_specs=[SMEM] * 2 + [HBM] * 13 + [VMEM] * 8,
        out_specs=(VMEM, VMEM, VMEM),
        scratch_shapes=[
            pltpu.VMEM((rows + 8, cols), F32),
            pltpu.VMEM((rows + TILE, x_cols), BF16),
            pltpu.VMEM((rows + TILE, 128), BF16),
            pltpu.VMEM((rows, 128), BF16),
            pltpu.VMEM((rows + TILE, 128), F32),
            pltpu.VMEM((rows + TILE, 128), F32),
        ]
        + weight_scratch(weights, 3 * block_rows, len(blocks))
        + [
            pltpu.VMEM((requests, state_size, x_cols), BF16),
            pltpu.SemaphoreType.DMA((requests,)),
            pltpu.VMEM((8 * PRIORS, x_cols), BF16),
            pltpu.SemaphoreType.DMA((2,)),
        ],
        compiler_params=pltpu.CompilerParams(vmem_limit_bytes=MOST),
        cost_estimate=pl.CostEstimate(flops=16000000000, bytes_accessed=18000000, transcendentals=2000000),
        name="mixer_inner",
    )(z, table, *blocks, *weights, *parts, *priors, *projected, info, columns, taps, bias, decay, skip)


def mixer_late(table, first, arrays, c_rows, fade, total, rows):
    x_cols = total.shape[0] * 128
    state_size, requests = c_rows.shape[1], table.shape[1] - 1
    return pl.pallas_call(
        lambda *refs: late_kernel(first, len(arrays), *refs),
        out_shape=jax.ShapeDtypeStruct((rows, x_cols), BF16),
        in_specs=[SMEM] + [HBM] * len(arrays) + [VMEM] * 2 + [HBM],
        out_specs=VMEM,
        scratch_shapes=[
            pltpu.VMEM((requests, state_size, x_cols), BF16),
            pltpu.VMEM(total.shape, F32),
            pltpu.SemaphoreType.DMA((requests,)),
            pltpu.SemaphoreType.DMA,
        ],
        compiler_params=pltpu.CompilerParams(vmem_limit_bytes=MOST),
        cost_estimate=pl.CostEstimate(flops=500000000, bytes_accessed=13000000, transcendentals=0),
        name="mixer_late",
    )(table, *arrays, c_rows, fade, total)


def shards(
    tokens, weight_x, weight_bc, weight_dt, kernel_x, kernel_bc, dt_bias, decay_rate, skip_gain,
    ssm_pool, conv_x_pool, conv_bc_pool, hit_holder, hit_slot, suffix_len,
):
    model_dim, heads = weight_dt.shape
    x_cols = weight_x.shape[1]
    bc_cols = weight_bc.shape[1] * weight_bc.shape[2]
    slots, head_size, state_size = ssm_pool.shape[0], ssm_pool.shape[2], ssm_pool.shape[3]
    requests = suffix_len.shape[1]
    me, z = lax.axis_index("cache"), lax.axis_index("tp")

    weights = (weight_x, weight_bc.reshape(model_dim, bc_cols), weight_dt.T)

    lengths = suffix_len[0]
    order = jnp.arange(requests, dtype=jnp.int32)
    ends = jnp.sum(jnp.where(order[None, :] <= order[:, None], lengths[None, :], 0), axis=1)
    starts = ends - lengths
    holder = lax.dynamic_slice_in_dim(hit_holder[:, 0], me * requests, requests)
    slot = lax.dynamic_slice_in_dim(hit_slot, me * requests, requests)
    my_y, my_x, my_c = me // (2 * NX), (me // 2) % NX, me % 2
    at_y, at_x, at_c = holder // (2 * NX), (holder // 2) % NX, holder % 2
    far_y, far_x = (my_y - at_y) % NY, (my_x - at_x) % NX
    outer, inner = jnp.where(at_c == 0, far_y, far_x), jnp.where(at_c == 0, far_x, far_y)
    node = jnp.where(inner == 2, 3, jnp.where(inner == 3, 2, inner))
    line = jnp.where(outer == 2, 3, jnp.where(outer == 3, 2, outer))
    prior_row = ((at_c != my_c) * NY + line) * PRIORS + node * PRIOR + slot * 3
    block = 2 * node + slot
    part_of = jnp.where(outer == 2, 3 + block // 4, line)
    block = jnp.where(outer == 2, block % 4, block)
    own = at_c == my_c
    array = jnp.where(
        part_of < 3,
        jnp.where(part_of == 0, jnp.where(own, 0, 1), jnp.where(own, 1, 3) + part_of),
        jnp.where(own, 0, 1) + 2 * part_of,
    )
    key = array * requests + order
    rank = jnp.sum((key[None, :] < key[:, None]).astype(jnp.int32), axis=1)
    sorting = (rank[None, :] == order[:, None]).astype(jnp.int32)
    by_array = jnp.sum(sorting[None] * jnp.stack([starts, lengths, block])[:, None, :], axis=2)
    firsts = jnp.sum((array[None, :] < order[:, None]).astype(jnp.int32), axis=1)
    table = jnp.concatenate([by_array, firsts[None]], axis=0).astype(jnp.int32)
    table = jnp.pad(table, ((0, 0), (0, 1)))
    info = jnp.stack([ends, starts])
    info = jnp.concatenate([info, jnp.full((2, 128 - requests), 1 << 20, jnp.int32)], axis=1)

    taps = jnp.concatenate([kernel_x, kernel_bc.reshape(4, bc_cols)], axis=1).astype(F32)
    pad = (0, 128 - heads)
    from_row = (prior_row[:, None] + jnp.arange(3)[None, :]).reshape(-1)
    from_row = jnp.pad(from_row, (0, 128 - 3 * requests), constant_values=-16)
    columns = jnp.stack([from_row, info[0]], axis=1)
    tables = (
        table, weights, info, columns, taps, jnp.pad(dt_bias, pad)[None], jnp.pad(decay_rate, pad)[None],
        jnp.repeat(skip_gain, head_size)[None],
    )

    def inner(blocks, projected, parts, priors, tables):
        table, weights, info, columns, taps, bias, decay, skip = tables
        sums = mixer_inner(
            z.reshape(1), table, blocks, weights, parts, priors, projected, info, columns, taps,
            bias, decay, skip,
        )
        return sums, table

    states = jnp.swapaxes(ssm_pool.reshape(slots, heads * head_size, state_size), 1, 2)
    conv_bc = jnp.pad(conv_bc_pool.reshape(slots * 3, bc_cols), ((0, PRIOR - 12), (0, x_cols - bc_cols)))
    pool = jnp.concatenate(
        [states.reshape(slots * state_size, x_cols), conv_x_pool.reshape(slots * 3, x_cols), conv_bc]
    )
    late, ((total, c_rows, fade), table) = gather(pool, tokens, tables, project, inner)
    return mixer_late(table, 4, late, c_rows, fade, total, NZ * tokens.shape[0])


def solution(mesh):
    in_specs = (
        P(("cache", "tp"), None), P(None, "tp"), P(None, None, "tp"), P(None, "tp"), P(None, "tp"),
        P(None, None, "tp"), P("tp"), P("tp"), P("tp"), P("cache", "tp", None, None), P("cache", None, "tp"),
        P("cache", None, None, "tp"), P(), P(), P("cache", None),
    )
    return jax.shard_map(
        shards, mesh=mesh, in_specs=in_specs, out_specs=P("cache", "tp"), check_vma=False
    )
```

profile of v0, /device:TPU:1, one launch (start us, length us, event | category | flops | bytes accessed | tf_op | source)
XLA Modules:
  0.0 123.4 jit_solution(17454751939967444475)
XLA Ops:
  0.0 2.5 %collective-permute-start.3 = (bf16[64,4096]{1,0:T(8,128)(2,1)}, bf16[64,4096]{1,0:T(8,128)(2,1)}, u32[]{:S(2)}, u32[]{:S(2)}) collective-permute-start(bf16[64,4096]{1,0:T(8,128)(2,1)} %refs_0_), channel_id=1, source_target_pairs={{0,1},{1,2},{2,3},{3,4},{4,5},{5,6},{6,7},{7,0},{8,9},{9,10},{10,1... | collective-permute-start | bytes 1572872 | tf_op jit(solution)/shard_map/ppermute | solution.py:37
  2.6 4.0 %collective-permute-start.4 = (bf16[64,4096]{1,0:T(8,128)(2,1)}, bf16[64,4096]{1,0:T(8,128)(2,1)}, u32[]{:S(2)}, u32[]{:S(2)}) collective-permute-start(bf16[64,4096]{1,0:T(8,128)(2,1)} %refs_0_), channel_id=1, source_target_pairs={{0,7},{1,0},{2,1},{3,2},{4,3},{5,4},{6,5},{7,6},{8,15},{9,8},{10,9... | collective-permute-start | bytes 1572872 | tf_op jit(solution)/shard_map/ppermute | solution.py:37
  8.0 1.2 %copy.27 = bf16[2,1024,128]{1,2,0:T(8,128)(2,1)S(1)} copy(bf16[2,1024,128]{2,1,0:T(8,128)(2,1)} %bitcast.70) | data formatting | bytes 1048576 | tf_op jit(solution)/shard_map/reshape | solution.py:518
  9.3 3.0 %collective-permute-start.2 = (bf16[272,1024]{1,0:T(8,128)(2,1)S(1)}, bf16[272,1024]{1,0:T(8,128)(2,1)S(1)}, u32[]{:S(2)}, u32[]{:S(2)}) collective-permute-start(bf16[272,1024]{1,0:T(8,128)(2,1)S(1)} %fusion.1.refs_0_), channel_id=1, source_target_pairs={{0,32},{8,136},{16,48},{24,152},{32,0},{40,168},{48,16},{56,184},{... | collective-permute-start | bytes 1671176 | tf_op jit(solution)/shard_map/ppermute | solution.py:41
  18.1 1.6 %copy.36 = bf16[512,8,2,128]{3,1,2,0:T(8,128)(2,1)} copy(bf16[512,8,2,128]{3,2,1,0:T(2,128)(2,1)S(1)} %bitcast.66) | data formatting | bytes 4194304
  20.9 5.1 %collective-permute-done.1.refs_2_ = bf16[272,1024]{1,0:T(8,128)(2,1)} collective-permute-done((bf16[272,1024]{1,0:T(8,128)(2,1)S(1)}, bf16[272,1024]{1,0:T(8,128)(2,1)}, u32[]{:S(2)}, u32[]{:S(2)}) %collective-permute-start.1) | collective-permute-done | bytes 557088 | tf_op jit(solution)/shard_map/ppermute | solution.py:41
  26.1 2.6 %lined.1 = (bf16[1024,1024]{1,0:T(8,128)(2,1)}, bf16[64,1024]{1,0:T(8,128)(2,1)}) custom-call(bf16[272,1024]{1,0:T(8,128)(2,1)} %copy-done, bf16[272,1024]{1,0:T(8,128)(2,1)} %collective-permute-done.refs_1_, bf16[272,1024]{1,0:T(8,128)(2,1)} %collective-permute-done.1.refs_2_, bf16[272,1024]{1,0:T(8,128)(2,1)} %copy-done.7), custom_call_target="tpu_custom_call" | custom-call | bytes 4000000 | tf_op jit(solution)/shard_map/lined/pallas_call | solution.py:62
  28.7 2.8 %collective-permute-start.7 = (bf16[64,1024]{1,0:T(8,128)(2,1)}, bf16[64,1024]{1,0:T(8,128)(2,1)S(1)}, u32[]{:S(2)}, u32[]{:S(2)}) collective-permute-start(bf16[64,1024]{1,0:T(8,128)(2,1)} %get-tuple-element.70.refs_0_), channel_id=1, source_target_pairs={{0,128},{8,40},{16,144},{24,56},{32,160},{40,8},{48,176},{56,24},{... | collective-permute-start | bytes 393224 | tf_op jit(solution)/shard_map/ppermute | solution.py:41
  33.0 1.3 %collective-permute-done.7.refs_3_ = bf16[64,1024]{1,0:T(8,128)(2,1)S(1)} collective-permute-done((bf16[64,1024]{1,0:T(8,128)(2,1)}, bf16[64,1024]{1,0:T(8,128)(2,1)S(1)}, u32[]{:S(2)}, u32[]{:S(2)}) %collective-permute-start.7) | collective-permute-done | bytes 131104 | tf_op jit(solution)/shard_map/ppermute | solution.py:41
  34.3 1.8 %collective-permute-done.6.refs_2_ = bf16[64,1024]{1,0:T(8,128)(2,1)S(1)} collective-permute-done((bf16[64,1024]{1,0:T(8,128)(2,1)}, bf16[64,1024]{1,0:T(8,128)(2,1)S(1)}, u32[]{:S(2)}, u32[]{:S(2)}) %collective-permute-start.6) | collective-permute-done | bytes 131104 | tf_op jit(solution)/shard_map/ppermute | solution.py:41
  36.1 1.5 %collective-permute-done.5.refs_1_ = bf16[64,1024]{1,0:T(8,128)(2,1)S(1)} collective-permute-done((bf16[64,1024]{1,0:T(8,128)(2,1)}, bf16[64,1024]{1,0:T(8,128)(2,1)S(1)}, u32[]{:S(2)}, u32[]{:S(2)}) %collective-permute-start.5) | collective-permute-done | bytes 131104 | tf_op jit(solution)/shard_map/ppermute | solution.py:41
  37.6 3.3 %collective-permute-start.14 = (bf16[1024,1024]{1,0:T(8,128)(2,1)}, bf16[1024,1024]{1,0:T(8,128)(2,1)}, u32[]{:S(2)}, u32[]{:S(2)}) collective-permute-start(bf16[1024,1024]{1,0:T(8,128)(2,1)} %get-tuple-element.67.s0), channel_id=1, source_target_pairs={{0,8},{8,0},{16,24},{24,16},{32,40},{40,32},{48,56},{56,48},{64,72... | collective-permute-start | bytes 6291464 | tf_op jit(solution)/shard_map/ppermute | solution.py:41
  41.0 2.3 %collective-permute-start.9 = (bf16[1024,1024]{1,0:T(8,128)(2,1)}, bf16[1024,1024]{1,0:T(8,128)(2,1)S(1)}, u32[]{:S(2)}, u32[]{:S(2)}) collective-permute-start(bf16[1024,1024]{1,0:T(8,128)(2,1)} %get-tuple-element.67.s0), channel_id=1, source_target_pairs={{0,192},{8,56},{16,208},{24,8},{32,224},{40,24},{48,240},{56,40},{... | collective-permute-start | bytes 6291464 | tf_op jit(solution)/shard_map/ppermute | solution.py:41
  43.4 2.7 %collective-permute-start.12 = (bf16[64,4096]{1,0:T(8,128)(2,1)}, bf16[64,4096]{1,0:T(8,128)(2,1)S(1)}, u32[]{:S(2)}, u32[]{:S(2)}) collective-permute-start(bf16[64,4096]{1,0:T(8,128)(2,1)} %collective-permute-done.4.refs_2_), channel_id=1, source_target_pairs={{0,7},{1,0},{2,1},{3,2},{4,3},{5,4},{6,5},{7,6},{8,15},{9,8},{10,9... | collective-permute-start | bytes 1572872 | tf_op jit(solution)/shard_map/ppermute | solution.py:37
  46.0 1.8 %stacked.1.p0 = bf16[256,1024]{1,0:T(8,128)(2,1)} custom-call(bf16[64,1024]{1,0:T(8,128)(2,1)} %get-tuple-element.70.refs_0_, bf16[64,1024]{1,0:T(8,128)(2,1)} %copy-done.12, bf16[64,1024]{1,0:T(8,128)(2,1)} %copy-done.11, bf16[64,1024]{1,0:T(8,128)(2,1)} %copy-done.10), custom_call_target="tpu_custom_call" | custom-call | bytes 4000000 | tf_op jit(solution)/shard_map/stacked/pallas_call | solution.py:62
  47.9 10.8 %collective-permute-done.10.refs_3_ = bf16[64,4096]{1,0:T(8,128)(2,1)} collective-permute-done((bf16[64,4096]{1,0:T(8,128)(2,1)}, bf16[64,4096]{1,0:T(8,128)(2,1)}, u32[]{:S(2)}, u32[]{:S(2)}) %collective-permute-start.10) | collective-permute-done | bytes 524320 | tf_op jit(solution)/shard_map/ppermute | solution.py:37
  60.0 0.9 collective-permute-done.15.p1
  61.0 1.2 collective-permute-start.13
  62.2 7.9 %project.1 = (bf16[320,1024]{1,0:T(8,128)(2,1)}, bf16[320,384]{1,0:T(8,128)(2,1)}) custom-call(bf16[64,4096]{1,0:T(8,128)(2,1)} %refs_0_, bf16[64,4096]{1,0:T(8,128)(2,1)} %collective-permute-done.3.refs_1_, bf16[64,4096]{1,0:T(8,128)(2,1)} %collective-permute-done.4.refs_2_, bf16[64,4096]{1,0:T(8,128)(2,1)} %collective-permute-done.10.refs_3_, ...), custom_call_target="tpu_custom_call" | custom-call | flops 8000000000 | bytes 14000000 | tf_op jit(solution)/shard_map/project/pallas_call | solution.py:386
  70.1 4.0 %collective-permute-done.11.refs_0_.b0 = bf16[64,4096]{1,0:T(8,128)(2,1)S(1)} collective-permute-done((bf16[64,4096]{1,0:T(8,128)(2,1)}, bf16[64,4096]{1,0:T(8,128)(2,1)S(1)}, u32[]{:S(2)}, u32[]{:S(2)}) %collective-permute-start.11) | collective-permute-done | bytes 524320 | tf_op jit(solution)/shard_map/ppermute | solution.py:37
  75.1 1.9 %halves.3 = (bf16[32,4096]{1,0:T(8,128)(2,1)}, bf16[32,4096]{1,0:T(8,128)(2,1)}) custom-call(bf16[64,4096]{1,0:T(8,128)(2,1)} %copy-done.8, bf16[64,4096]{1,0:T(8,128)(2,1)} %copy-done.9), custom_call_target="tpu_custom_call" | custom-call | bytes 4000000 | tf_op jit(solution)/shard_map/halves/pallas_call | solution.py:62
  77.0 1.2 collective-permute-start.18
  78.2 1.6 %collective-permute-start.19 = (bf16[32,4096]{1,0:T(8,128)(2,1)}, bf16[32,4096]{1,0:T(8,128)(2,1)S(1)}, u32[]{:S(2)}, u32[]{:S(2)}) collective-permute-start(bf16[32,4096]{1,0:T(8,128)(2,1)} %get-tuple-element.92), channel_id=1, source_target_pairs={{0,7},{1,0},{2,1},{3,2},{4,3},{5,4},{6,5},{7,6},{8,15},{9,8},{10,9... | collective-permute-start | bytes 786440 | tf_op jit(solution)/shard_map/ppermute | solution.py:37
  80.5 2.6 %halves.2 = (bf16[512,1024]{1,0:T(8,128)(2,1)}, bf16[512,1024]{1,0:T(8,128)(2,1)}) custom-call(bf16[1024,1024]{1,0:T(8,128)(2,1)} %collective-permute-done.8.refs_0_.s2, bf16[1024,1024]{1,0:T(8,128)(2,1)} %copy-done.3), custom_call_target="tpu_custom_call" | custom-call | bytes 4000000 | tf_op jit(solution)/shard_map/halves/pallas_call | solution.py:62
  83.5 2.5 %collective-permute-start.17 = (bf16[512,1024]{1,0:T(8,128)(2,1)}, bf16[512,1024]{1,0:T(8,128)(2,1)}, u32[]{:S(2)}, u32[]{:S(2)}) collective-permute-start(bf16[512,1024]{1,0:T(8,128)(2,1)} %get-tuple-element.87), channel_id=1, source_target_pairs={{0,192},{8,56},{16,208},{24,8},{32,224},{40,24},{48,240},{56,40},{... | collective-permute-start | bytes 3145736 | tf_op jit(solution)/shard_map/ppermute | solution.py:41
  86.0 2.3 %collective-permute-start.20 = (bf16[1024,1024]{1,0:T(8,128)(2,1)}, bf16[1024,1024]{1,0:T(8,128)(2,1)S(1)}, u32[]{:S(2)}, u32[]{:S(2)}) collective-permute-start(bf16[1024,1024]{1,0:T(8,128)(2,1)} %collective-permute-done.8.refs_0_.s2), channel_id=1, source_target_pairs={{0,8},{8,0},{16,24},{24,16},{32,40},{40,32},{48,56},{56,48},{64,72... | collective-permute-start | bytes 6291464 | tf_op jit(solution)/shard_map/ppermute | solution.py:41
  88.4 21.7 %mixer_inner.1 = (f32[8,544,128]{2,1,0:T(8,128)}, f32[544,128]{1,0:T(8,128)}, f32[544,128]{1,0:T(8,128)}) custom-call(s32[1]{0:T(128)} %bitcast.13.where, s32[4,33]{1,0:T(4,128)} %pad.21.table.refs_0_, bf16[64,4096]{1,0:T(8,128)(2,1)} %copy-done.8, bf16[64,4096]{1,0:T(8,128)(2,1)} %copy-done.9, bf16[32,4096]{1,0:T(8,128)(2,1)} %copy-done.21, ...), custom_call_target="tpu_custom_call" | custom-call | flops 16000000000 | bytes 18000000 | tf_op jit(solution)/shard_map/mixer_inner/pallas_call | solution.py:405
  110.8 2.7 %collective-permute-done.22.refs_4_ = bf16[512,1024]{1,0:T(8,128)(2,1)S(1)} collective-permute-done((bf16[512,1024]{1,0:T(8,128)(2,1)S(1)}, bf16[512,1024]{1,0:T(8,128)(2,1)S(1)}, u32[]{:S(2)}, u32[]{:S(2)}) %collective-permute-start.22) | collective-permute-done | bytes 1048608 | tf_op jit(solution)/shard_map/ppermute | solution.py:41
  113.5 1.2 collective-permute-done.23.refs_6_
  114.7 1.0 copy-done.6
  115.7 1.4 %copy-done.1 = bf16[1024,1024]{1,0:T(8,128)(2,1)} copy-done((bf16[1024,1024]{1,0:T(8,128)(2,1)}, bf16[1024,1024]{1,0:T(8,128)(2,1)S(1)}, u32[]{:S(2)}) %copy-start.1) | copy-done | bytes 2097176
  117.1 6.1 %mixer_late.1 = bf16[512,1024]{1,0:T(8,128)(2,1)} custom-call(s32[4,33]{1,0:T(4,128)} %pad.21.table.refs_0_, bf16[1024,1024]{1,0:T(8,128)(2,1)} %copy-done.1, bf16[1024,1024]{1,0:T(8,128)(2,1)} %collective-permute-done.21.refs_2_, bf16[512,1024]{1,0:T(8,128)(2,1)} %copy-done.4, bf16[512,1024]{1,0:T(8,128)(2,1)} %copy-done.5, ...), custom_call_target="tpu_custom_call" | custom-call | flops 500000000 | bytes 13000000 | tf_op jit(solution)/shard_map/mixer_late/pallas_call | solution.py:438
  (98 shorter events, 14.1 us)
Async XLA Ops:
  0.0 13.8 %copy-start.15 = (s32[1,32]{1,0:T(1,128)S(1)}, s32[1,32]{1,0:T(1,128)}, u32[]{:S(2)}) copy-start(s32[1,32]{1,0:T(1,128)} %param.29) | copy-start | bytes 388
  0.0 16.1 %copy-start.14 = (bf16[4,2,128]{2,1,0:T(2,128)(2,1)S(1)}, bf16[4,2,128]{2,1,0:T(2,128)(2,1)}, u32[]{:S(2)}) copy-start(bf16[4,2,128]{2,1,0:T(2,128)(2,1)} %param.20) | copy-start | bytes 6148
  0.0 16.1 %copy-start.16 = (f32[16]{0:T(128)S(1)}, f32[16]{0:T(128)}, u32[]{:S(2)}) copy-start(f32[16]{0:T(128)} %param.23) | copy-start | bytes 196
  0.0 18.0 %copy-start.2 = (bf16[4096,2,128]{2,1,0:T(2,128)(2,1)S(1)}, bf16[4096,2,128]{2,1,0:T(2,128)(2,1)}, u32[]{:S(2)}) copy-start(bf16[4096,2,128]{2,1,0:T(2,128)(2,1)} %param.17) | copy-start | bytes 6291460
  0.0 20.9 %collective-permute-start.3 = (bf16[64,4096]{1,0:T(8,128)(2,1)}, bf16[64,4096]{1,0:T(8,128)(2,1)}, u32[]{:S(2)}, u32[]{:S(2)}) collective-permute-start(bf16[64,4096]{1,0:T(8,128)(2,1)} %refs_0_), channel_id=1, source_target_pairs={{0,1},{1,2},{2,3},{3,4},{4,5},{5,6},{6,7},{7,0},{8,9},{9,10},{10,1... | collective-permute-start | bytes 1572872 | tf_op jit(solution)/shard_map/ppermute | solution.py:37
  2.6 18.4 %collective-permute-start.4 = (bf16[64,4096]{1,0:T(8,128)(2,1)}, bf16[64,4096]{1,0:T(8,128)(2,1)}, u32[]{:S(2)}, u32[]{:S(2)}) collective-permute-start(bf16[64,4096]{1,0:T(8,128)(2,1)} %refs_0_), channel_id=1, source_target_pairs={{0,7},{1,0},{2,1},{3,2},{4,3},{5,4},{6,5},{7,6},{8,15},{9,8},{10,9... | collective-permute-start | bytes 1572872 | tf_op jit(solution)/shard_map/ppermute | solution.py:37
  9.3 10.4 %copy-start = (bf16[272,1024]{1,0:T(8,128)(2,1)}, bf16[272,1024]{1,0:T(8,128)(2,1)S(1)}, u32[]{:S(2)}) copy-start(bf16[272,1024]{1,0:T(8,128)(2,1)S(1)} %fusion.1.refs_0_) | copy-start | bytes 1671172
  9.3 11.6 %collective-permute-start.2 = (bf16[272,1024]{1,0:T(8,128)(2,1)S(1)}, bf16[272,1024]{1,0:T(8,128)(2,1)S(1)}, u32[]{:S(2)}, u32[]{:S(2)}) collective-permute-start(bf16[272,1024]{1,0:T(8,128)(2,1)S(1)} %fusion.1.refs_0_), channel_id=1, source_target_pairs={{0,32},{8,136},{16,48},{24,152},{32,0},{40,168},{48,16},{56,184},{... | collective-permute-start | bytes 1671176 | tf_op jit(solution)/shard_map/ppermute | solution.py:41
  12.3 13.7 %collective-permute-start.1 = (bf16[272,1024]{1,0:T(8,128)(2,1)S(1)}, bf16[272,1024]{1,0:T(8,128)(2,1)}, u32[]{:S(2)}, u32[]{:S(2)}) collective-permute-start(bf16[272,1024]{1,0:T(8,128)(2,1)S(1)} %fusion.1.refs_0_), channel_id=1, source_target_pairs={{0,48},{8,200},{16,0},{24,216},{32,16},{40,232},{48,32},{56,248},{... | collective-permute-start | bytes 1671176 | tf_op jit(solution)/shard_map/ppermute | solution.py:41
  13.1 13.0 %collective-permute-start = (bf16[272,1024]{1,0:T(8,128)(2,1)S(1)}, bf16[272,1024]{1,0:T(8,128)(2,1)}, u32[]{:S(2)}, u32[]{:S(2)}) collective-permute-start(bf16[272,1024]{1,0:T(8,128)(2,1)S(1)} %fusion.1.refs_0_), channel_id=1, source_target_pairs={{0,16},{8,72},{16,32},{24,88},{32,48},{40,104},{48,0},{56,120},{64... | collective-permute-start | bytes 1671176 | tf_op jit(solution)/shard_map/ppermute | solution.py:41
  28.7 5.6 %collective-permute-start.7 = (bf16[64,1024]{1,0:T(8,128)(2,1)}, bf16[64,1024]{1,0:T(8,128)(2,1)S(1)}, u32[]{:S(2)}, u32[]{:S(2)}) collective-permute-start(bf16[64,1024]{1,0:T(8,128)(2,1)} %get-tuple-element.70.refs_0_), channel_id=1, source_target_pairs={{0,128},{8,40},{16,144},{24,56},{32,160},{40,8},{48,176},{56,24},{... | collective-permute-start | bytes 393224 | tf_op jit(solution)/shard_map/ppermute | solution.py:41
  31.5 4.6 %collective-permute-start.6 = (bf16[64,1024]{1,0:T(8,128)(2,1)}, bf16[64,1024]{1,0:T(8,128)(2,1)S(1)}, u32[]{:S(2)}, u32[]{:S(2)}) collective-permute-start(bf16[64,1024]{1,0:T(8,128)(2,1)} %get-tuple-element.70.refs_0_), channel_id=1, source_target_pairs={{0,192},{8,56},{16,208},{24,8},{32,224},{40,24},{48,240},{56,40},{... | collective-permute-start | bytes 393224 | tf_op jit(solution)/shard_map/ppermute | solution.py:41
  32.4 5.2 %collective-permute-start.5 = (bf16[64,1024]{1,0:T(8,128)(2,1)}, bf16[64,1024]{1,0:T(8,128)(2,1)S(1)}, u32[]{:S(2)}, u32[]{:S(2)}) collective-permute-start(bf16[64,1024]{1,0:T(8,128)(2,1)} %get-tuple-element.70.refs_0_), channel_id=1, source_target_pairs={{0,64},{8,24},{16,80},{24,40},{32,96},{40,56},{48,112},{56,8},{64,... | collective-permute-start | bytes 393224 | tf_op jit(solution)/shard_map/ppermute | solution.py:41
  34.3 11.7 %copy-start.10 = (bf16[64,1024]{1,0:T(8,128)(2,1)}, bf16[64,1024]{1,0:T(8,128)(2,1)S(1)}, u32[]{:S(2)}) copy-start(bf16[64,1024]{1,0:T(8,128)(2,1)S(1)} %collective-permute-done.7.refs_3_) | copy-start | bytes 393220
  36.1 9.9 %copy-start.11 = (bf16[64,1024]{1,0:T(8,128)(2,1)}, bf16[64,1024]{1,0:T(8,128)(2,1)S(1)}, u32[]{:S(2)}) copy-start(bf16[64,1024]{1,0:T(8,128)(2,1)S(1)} %collective-permute-done.6.refs_2_) | copy-start | bytes 393220
  37.6 24.5 %collective-permute-start.14 = (bf16[1024,1024]{1,0:T(8,128)(2,1)}, bf16[1024,1024]{1,0:T(8,128)(2,1)}, u32[]{:S(2)}, u32[]{:S(2)}) collective-permute-start(bf16[1024,1024]{1,0:T(8,128)(2,1)} %get-tuple-element.67.s0), channel_id=1, source_target_pairs={{0,8},{8,0},{16,24},{24,16},{32,40},{40,32},{48,56},{56,48},{64,72... | collective-permute-start | bytes 6291464 | tf_op jit(solution)/shard_map/ppermute | solution.py:41
  41.0 33.3 %collective-permute-start.9 = (bf16[1024,1024]{1,0:T(8,128)(2,1)}, bf16[1024,1024]{1,0:T(8,128)(2,1)S(1)}, u32[]{:S(2)}, u32[]{:S(2)}) collective-permute-start(bf16[1024,1024]{1,0:T(8,128)(2,1)} %get-tuple-element.67.s0), channel_id=1, source_target_pairs={{0,192},{8,56},{16,208},{24,8},{32,224},{40,24},{48,240},{56,40},{... | collective-permute-start | bytes 6291464 | tf_op jit(solution)/shard_map/ppermute | solution.py:41
  43.3 31.0 %collective-permute-start.8 = (bf16[1024,1024]{1,0:T(8,128)(2,1)}, bf16[1024,1024]{1,0:T(8,128)(2,1)}, u32[]{:S(2)}, u32[]{:S(2)}) collective-permute-start(bf16[1024,1024]{1,0:T(8,128)(2,1)} %get-tuple-element.67.s0), channel_id=1, source_target_pairs={{0,64},{8,24},{16,80},{24,40},{32,96},{40,56},{48,112},{56,8},{64,... | collective-permute-start | bytes 6291464 | tf_op jit(solution)/shard_map/ppermute | solution.py:41
  43.3 15.3 %collective-permute-start.10 = (bf16[64,4096]{1,0:T(8,128)(2,1)}, bf16[64,4096]{1,0:T(8,128)(2,1)}, u32[]{:S(2)}, u32[]{:S(2)}) collective-permute-start(bf16[64,4096]{1,0:T(8,128)(2,1)} %collective-permute-done.3.refs_1_), channel_id=1, source_target_pairs={{0,1},{1,2},{2,3},{3,4},{4,5},{5,6},{6,7},{7,0},{8,9},{9,10},{10,1... | collective-permute-start | bytes 1572872 | tf_op jit(solution)/shard_map/ppermute | solution.py:37
  43.4 15.9 %collective-permute-start.12 = (bf16[64,4096]{1,0:T(8,128)(2,1)}, bf16[64,4096]{1,0:T(8,128)(2,1)S(1)}, u32[]{:S(2)}, u32[]{:S(2)}) collective-permute-start(bf16[64,4096]{1,0:T(8,128)(2,1)} %collective-permute-done.4.refs_2_), channel_id=1, source_target_pairs={{0,7},{1,0},{2,1},{3,2},{4,3},{5,4},{6,5},{7,6},{8,15},{9,8},{10,9... | collective-permute-start | bytes 1572872 | tf_op jit(solution)/shard_map/ppermute | solution.py:37
  58.7 2.3 %collective-permute-start.15 = (bf16[256,1024]{1,0:T(8,128)(2,1)}, bf16[256,1024]{1,0:T(8,128)(2,1)S(1)}, u32[]{:S(2)}, u32[]{:S(2)}) collective-permute-start(bf16[256,1024]{1,0:T(8,128)(2,1)} %stacked.1.p0), channel_id=1, source_target_pairs={{0,8},{8,0},{16,24},{24,16},{32,40},{40,32},{48,56},{56,48},{64,72... | collective-permute-start | bytes 1572872 | tf_op jit(solution)/shard_map/ppermute | solution.py:41
  59.2 14.9 %collective-permute-start.11 = (bf16[64,4096]{1,0:T(8,128)(2,1)}, bf16[64,4096]{1,0:T(8,128)(2,1)S(1)}, u32[]{:S(2)}, u32[]{:S(2)}) collective-permute-start(bf16[64,4096]{1,0:T(8,128)(2,1)} %collective-permute-done.10.refs_3_), channel_id=1, source_target_pairs={{0,1},{1,2},{2,3},{3,4},{4,5},{5,6},{6,7},{7,0},{8,9},{9,10},{10,1... | collective-permute-start | bytes 1572872 | tf_op jit(solution)/shard_map/ppermute | solution.py:37
  61.0 9.1 %copy-start.19 = (bf16[256,1024]{1,0:T(8,128)(2,1)}, bf16[256,1024]{1,0:T(8,128)(2,1)S(1)}, u32[]{:S(2)}) copy-start(bf16[256,1024]{1,0:T(8,128)(2,1)S(1)} %collective-permute-done.15.p1) | copy-start | bytes 1572868
  61.0 13.3 %collective-permute-start.13 = (bf16[64,4096]{1,0:T(8,128)(2,1)}, bf16[64,4096]{1,0:T(8,128)(2,1)S(1)}, u32[]{:S(2)}, u32[]{:S(2)}) collective-permute-start(bf16[64,4096]{1,0:T(8,128)(2,1)} %copy-done.20), channel_id=1, source_target_pairs={{0,7},{1,0},{2,1},{3,2},{4,3},{5,4},{6,5},{7,6},{8,15},{9,8},{10,9... | collective-permute-start | bytes 1572872 | tf_op jit(solution)/shard_map/ppermute | solution.py:37
  77.0 8.9 %collective-permute-start.18 = (bf16[32,4096]{1,0:T(8,128)(2,1)}, bf16[32,4096]{1,0:T(8,128)(2,1)S(1)}, u32[]{:S(2)}, u32[]{:S(2)}) collective-permute-start(bf16[32,4096]{1,0:T(8,128)(2,1)} %get-tuple-element.91), channel_id=1, source_target_pairs={{0,1},{1,2},{2,3},{3,4},{4,5},{5,6},{6,7},{7,0},{8,9},{9,10},{10,1... | collective-permute-start | bytes 786440 | tf_op jit(solution)/shard_map/ppermute | solution.py:37
  78.2 7.8 %collective-permute-start.19 = (bf16[32,4096]{1,0:T(8,128)(2,1)}, bf16[32,4096]{1,0:T(8,128)(2,1)S(1)}, u32[]{:S(2)}, u32[]{:S(2)}) collective-permute-start(bf16[32,4096]{1,0:T(8,128)(2,1)} %get-tuple-element.92), channel_id=1, source_target_pairs={{0,7},{1,0},{2,1},{3,2},{4,3},{5,4},{6,5},{7,6},{8,15},{9,8},{10,9... | collective-permute-start | bytes 786440 | tf_op jit(solution)/shard_map/ppermute | solution.py:37
  83.1 27.0 %collective-permute-start.16 = (bf16[512,1024]{1,0:T(8,128)(2,1)}, bf16[512,1024]{1,0:T(8,128)(2,1)S(1)}, u32[]{:S(2)}, u32[]{:S(2)}) collective-permute-start(bf16[512,1024]{1,0:T(8,128)(2,1)} %get-tuple-element.86), channel_id=1, source_target_pairs={{0,64},{8,24},{16,80},{24,40},{32,96},{40,56},{48,112},{56,8},{64,... | collective-permute-start | bytes 3145736 | tf_op jit(solution)/shard_map/ppermute | solution.py:41
  83.5 26.7 %collective-permute-start.17 = (bf16[512,1024]{1,0:T(8,128)(2,1)}, bf16[512,1024]{1,0:T(8,128)(2,1)}, u32[]{:S(2)}, u32[]{:S(2)}) collective-permute-start(bf16[512,1024]{1,0:T(8,128)(2,1)} %get-tuple-element.87), channel_id=1, source_target_pairs={{0,192},{8,56},{16,208},{24,8},{32,224},{40,24},{48,240},{56,40},{... | collective-permute-start | bytes 3145736 | tf_op jit(solution)/shard_map/ppermute | solution.py:41
  86.0 28.8 %collective-permute-start.20 = (bf16[1024,1024]{1,0:T(8,128)(2,1)}, bf16[1024,1024]{1,0:T(8,128)(2,1)S(1)}, u32[]{:S(2)}, u32[]{:S(2)}) collective-permute-start(bf16[1024,1024]{1,0:T(8,128)(2,1)} %collective-permute-done.8.refs_0_.s2), channel_id=1, source_target_pairs={{0,8},{8,0},{16,24},{24,16},{32,40},{40,32},{48,56},{56,48},{64,72... | collective-permute-start | bytes 6291464 | tf_op jit(solution)/shard_map/ppermute | solution.py:41
  88.3 27.4 %collective-permute-start.21 = (bf16[1024,1024]{1,0:T(8,128)(2,1)}, bf16[1024,1024]{1,0:T(8,128)(2,1)}, u32[]{:S(2)}, u32[]{:S(2)}) collective-permute-start(bf16[1024,1024]{1,0:T(8,128)(2,1)} %copy-done.3), channel_id=1, source_target_pairs={{0,8},{8,0},{16,24},{24,16},{32,40},{40,32},{48,56},{56,48},{64,72... | collective-permute-start | bytes 6291464 | tf_op jit(solution)/shard_map/ppermute | solution.py:41
  110.1 3.4 %collective-permute-start.22 = (bf16[512,1024]{1,0:T(8,128)(2,1)S(1)}, bf16[512,1024]{1,0:T(8,128)(2,1)S(1)}, u32[]{:S(2)}, u32[]{:S(2)}) collective-permute-start(bf16[512,1024]{1,0:T(8,128)(2,1)S(1)} %collective-permute-done.16.refs_3_), channel_id=1, source_target_pairs={{0,8},{8,0},{16,24},{24,16},{32,40},{40,32},{48,56},{56,48},{64,72... | collective-permute-start | bytes 3145736 | tf_op jit(solution)/shard_map/ppermute | solution.py:41
  110.7 4.0 %collective-permute-start.23 = (bf16[512,1024]{1,0:T(8,128)(2,1)}, bf16[512,1024]{1,0:T(8,128)(2,1)S(1)}, u32[]{:S(2)}, u32[]{:S(2)}) collective-permute-start(bf16[512,1024]{1,0:T(8,128)(2,1)} %collective-permute-done.17.refs_5_), channel_id=1, source_target_pairs={{0,8},{8,0},{16,24},{24,16},{32,40},{40,32},{48,56},{56,48},{64,72... | collective-permute-start | bytes 3145736 | tf_op jit(solution)/shard_map/ppermute | solution.py:41
  (15 other events, 41.8 us)
where the time goes:
time: 125 us; the launch traced here: 123 us
  Pallas kernels  44.6 us (36%)
  starting transfers between devices  34.2 us (27%)
  waiting for transfers between devices  29.7 us (24%)
  local copies, waits for them, and re-layouts  11.7 us (9%)
  other arithmetic  2.8 us (2%)
    pallas_call x1, Pallas kernels, mixer_inner(): pl.pallas_call(inner_kernel, out_shape=(jax.ShapeDtypeStruct((x_cols // 1...  21.7 us
    ppermute x16, starting transfers between devices, on_cache(): return lax.ppermute(value, 'cache', pairs)  20.9 us
    ppermute x8, waiting for transfers between devices, over_z(): return lax.ppermute(value, 'tp', [(z, (z + step) % NZ) for z in range(NZ)])  15.1 us
    ppermute x16, waiting for transfers between devices, on_cache(): return lax.ppermute(value, 'cache', pairs)  14.6 us
    ppermute x8, starting transfers between devices, over_z(): return lax.ppermute(value, 'tp', [(z, (z + step) % NZ) for z in range(NZ)])  13.2 us
    pallas_call x4, Pallas kernels, moved(): pl.pallas_call(kernel, out_shape=[jax.ShapeDtypeStruct(shape, sources[0]....  8.93 us
    pallas_call x1, Pallas kernels, project(): pl.pallas_call(project_kernel, out_shape=(jax.ShapeDtypeStruct((rows, x_c...  7.89 us
    unnamed x50, local copies, waits for them, and re-layouts  7.08 us
  transfers between devices with their start and end apart: 24, of which 10 were waited for; matrix products, arithmetic and copies ran while one was open for 8% of the time, Pallas kernels for 28%

commit v1 on v0

--- a/solution.py
+++ b/solution.py
@@ -79,18 +79,19 @@
     moves = []
     for k in range(len(nodes)):
         moves.append((k, 0, states, 0, k * states))
+        moves.append((k, states, PRIOR, 0, len(nodes) * states + k * PRIOR))
         moves.append((k, states, PRIOR, 1, k * PRIOR))
-    return moved("lined", nodes, [(len(nodes) * states, cols), (len(nodes) * PRIOR, cols)], moves)
-
-
-def stacked(parts):
-    rows, cols = parts[0].shape
-    moves = [(k, 0, rows, 0, k * rows) for k in range(len(parts))]
-    return moved("stacked", parts, [(len(parts) * rows, cols)], moves)[0]
-
-
-def halves(top, bottom):
-    rows, cols = top.shape[0] // 2, top.shape[1]
+    shapes = [(len(nodes) * (states + PRIOR), cols), (len(nodes) * PRIOR, cols)]
+    return moved("lined", nodes, shapes, moves)
+
+
+def gathered_priors(lines):
+    moves = [(k, line.shape[0] - PRIORS, PRIORS, 0, k * PRIORS) for k, line in enumerate(lines)]
+    return moved("gathered_priors", lines, [(len(lines) * PRIORS, lines[0].shape[1])], moves)[0]
+
+
+def halves(top, bottom, spare=0):
+    rows, cols = (top.shape[0] - spare) // 2, top.shape[1]
     return moved("halves", [top, bottom], [(rows, cols)] * 2, [(0, 0, rows, 0, 0), (1, rows, rows, 1, 0)])
 
 
@@ -99,31 +100,31 @@
     near_up, near_down = on_cache(pool, first_round(1)), on_cache(pool, first_round(-1))
     far = on_cache(pool, first_round(2))
     up, down = over_z(tokens, 1), over_z(tokens, -1)
-    near_up, near_down, far, up, down, tables = tie((near_up, near_down, far, up, down, tables))
-
     blocks = [tokens, up, down]
     up, down = over_z(up, 1), over_z(down, -1)
     blocks += [up, down]
+    near_up, near_down, far, tables = tie((near_up, near_down, far, tables))
     line, line_prior = lined([pool, near_up, near_down, far])
-    priors = [line_prior] + [on_cache(line_prior, second_round(step)) for step in (1, -1, 2)]
-    line, priors = tie((line, priors))
+    line, line_prior, up, down, blocks = tie((line, line_prior, up, down, blocks))
+
     near_up, near_down = on_cache(line, second_round(1)), on_cache(line, second_round(-1))
-    priors = stacked(priors)
+    far_prior = on_cache(line_prior, second_round(2))
+    line_other = on_cache(line, CORES)
+    projected = [project(blocks, tables[1])]
+    up, down = over_z(up, 1), over_z(down, -1)
+    up, down, projected = tie((up, down, projected))
+    last_up, last_down = halves(up, down)
+    blocks = [up, down, over_z(last_up, 1), over_z(last_down, -1)]
+    blocks, line_other = tie((blocks, line_other))
+    projected.append(project(blocks, tables[1]))
+    near_up, near_down, far_prior, projected = tie((near_up, near_down, far_prior, projected))
+
+    priors = gathered_priors([line_prior, near_up, near_down, far_prior])
     priors = [priors, on_cache(priors, CORES)]
-    line_other = on_cache(line, CORES)
-    blocks, line_other, priors = tie((blocks, line_other, priors))
-    projected = project(blocks, tables[1])
-    up, down = over_z(up, 1), over_z(down, -1)
-    blocks = [up, down]
-    near_up, near_down, up, down, projected = tie((near_up, near_down, up, down, projected))
-
-    last_up, last_down = halves(up, down)
-    blocks += [over_z(last_up, 1), over_z(last_down, -1)]
-    far_up, far_down = halves(near_up, near_down)
+    far_up, far_down = halves(near_up, near_down, PRIORS)
     far_up, far_down = on_cache(far_up, second_round(1)), on_cache(far_down, second_round(-1))
-    up_other, down_other, blocks = tie((near_up, near_down, blocks))
-    up_other, down_other = on_cache(up_other, CORES), on_cache(down_other, CORES)
-    result = inner(blocks, projected, [line, line_other, near_up, near_down], priors, tables)
+    up_other, down_other = on_cache(near_up, CORES), on_cache(near_down, CORES)
+    result = inner(projected, [line, line_other, near_up, near_down], priors, tables)
     far_up, far_down, result = tie((far_up, far_down, result))
     far_others = [on_cache(far_up, CORES), on_cache(far_down, CORES)]
     return [up_other, down_other, far_up, far_others[0], far_down, far_others[1]], result
@@ -171,16 +172,16 @@
 
 
 def inner_kernel(
-    where, table, b0, b1, b2, b3, w_x_in, w_bc_in, w_dt_in, s0, s1, s2, s3, p0, p1,
-    x_first, b_first, info, cols_in, taps, bias, decay, skip, sum_ref, c_ref, fade_ref,
-    raw, xs, bs, cs, run, step, tok, w_x, w_bc, w_dt, sem, states, state_sem, prior, prior_sem,
+    where, table, s0, s1, s2, s3, p0, p1, x_first, b_first, x_next, b_next, info, cols_in, taps, bias, decay, skip, sum_ref,
+    raw, xs, bs, cs, run, step, states, state_sem, prior, prior_sem,
 ):
     rows = raw.shape[0] - 8
-    x_cols = w_x.shape[1]
+    x_cols = xs.shape[1]
+    c_ref, fade_ref = sum_ref.at[x_cols // 128], sum_ref.at[x_cols // 128 + 1]
     cols = taps.shape[1]
     block = rows // NZ
     z = where[0]
-    now, chunks = fetched([b0, b1, b2, b3], (w_x_in, w_bc_in, w_dt_in), tok, (w_x, w_bc, w_dt), sem)
+    now = []
     parts = (s0, s1, s2, s3)
     fetch_states(table, 0, parts, states, state_sem)
     for k, source in enumerate((p0, p1)):
@@ -196,6 +197,9 @@
     put(raw, 8, slice(0, x_cols), x_first, (0, -1, 1, -2, 2))
     put(raw, 8, slice(x_cols, cols), b_first[:, 0:256], (0, -1, 1, -2, 2))
     put(step, TILE, slice(None), b_first[:, 256:384], (0, -1, 1, -2, 2))
+    put(raw, 8, slice(0, x_cols), x_next, (-3, 3, 4))
+    put(raw, 8, slice(x_cols, cols), b_next[:, 0:256], (-3, 3, 4))
+    put(step, TILE, slice(None), b_next[:, 256:384], (-3, 3, 4))
     raw[0:8, :] = jnp.zeros((8, cols), F32)
 
     position = lax.broadcasted_iota(jnp.int32, (rows, 128), 0)
@@ -238,8 +242,6 @@
 
     for copy in now:
         copy.wait()
-    put(raw, 8, slice(x_cols, cols), dot(tok[...], w_bc[...]).astype(BF16), (-3, 3, 4))
-    put(step, TILE, slice(None), dot_t(tok[...], w_dt[...]).astype(BF16), (-3, 3, 4))
     out = convolved(slice(x_cols, cols), dot(pick_bc, prior[:, 0 : cols - x_cols]).astype(BF16))
     inputs = dot(pick_x, prior[...]).astype(BF16)
     bs[TILE:, :] = out[:, 0:128]
@@ -256,12 +258,8 @@
     run[TILE:, :] = running
     fade_ref[0:rows, :] = jnp.exp(running)
 
-    for k, copy in enumerate(chunks):
-        copy.wait()
-        here = slice(WIDE * k, WIDE * (k + 1))
-        put(raw, 8, here, dot(tok[...], w_x[:, here]).astype(BF16), (-3, 3, 4))
-        for at in range(WIDE * k, WIDE * (k + 1), 256):
-            xs[TILE:, at : at + 256] = convolved(slice(at, at + 256), inputs[:, at : at + 256])
+    for at in range(0, x_cols, 256):
+        xs[TILE:, at : at + 256] = convolved(slice(at, at + 256), inputs[:, at : at + 256])
 
     lanes = lax.broadcasted_iota(jnp.int32, (TILE, 2 * TILE), 1)
     subs = lax.broadcasted_iota(jnp.int32, (TILE, 2 * TILE), 0)
@@ -295,7 +293,7 @@
         return carry
 
     lax.fori_loop(0, rows // TILE, tile, 0)
-    sum_ref[:, rows:, :] = jnp.zeros((x_cols // 128, sum_ref.shape[1] - rows, 128), F32)
+    sum_ref[0 : x_cols // 128, rows:, :] = jnp.zeros((x_cols // 128, sum_ref.shape[1] - rows, 128), F32)
     fade_ref[rows:, :] = jnp.zeros((fade_ref.shape[0] - rows, 128), F32)
     add_carried(table, 0, parts, c_ref, fade_ref, states, sum_ref, state_sem)
 
@@ -354,20 +352,22 @@
 
 
 def late_kernel(first, count, table, *refs):
-    arrays, (c_ref, fade_ref, before, out, states, total, sems, got) = refs[:count], refs[count:]
-    rows = out.shape[0]
+    arrays, (before, out, states, total, sems, got) = refs[:count], refs[count:]
+    rows, x_cols = out.shape
+    c_ref, fade_ref = total.at[x_cols // 128], total.at[x_cols // 128 + 1]
     copy = pltpu.make_async_copy(before, total, got)
     copy.start()
     fetch_states(table, first, arrays, states, sems)
     copy.wait()
     add_carried(table, first, arrays, c_ref, fade_ref, states, total, sems)
-    for k in range(total.shape[0]):
+    for k in range(x_cols // 128):
         out[:, 128 * k : 128 * (k + 1)] = total[k, 0:rows, :].astype(BF16)
 
 
 VMEM = pl.BlockSpec(memory_space=pltpu.VMEM)
 SMEM = pl.BlockSpec(memory_space=pltpu.SMEM)
 HBM = pl.BlockSpec(memory_space=pltpu.HBM)
+ANY = pl.BlockSpec(memory_space=pl.ANY)
 
 
 def weight_scratch(weights, rows, copies):
@@ -398,19 +398,15 @@
     )(*blocks, *weights)
 
 
-def mixer_inner(z, table, blocks, weights, parts, priors, projected, info, columns, taps, bias, decay, skip):
-    block_rows = blocks[0].shape[0]
-    rows, x_cols, cols = NZ * block_rows, weights[0].shape[1], taps.shape[1]
+def mixer_inner(z, table, parts, priors, projected, info, columns, taps, bias, decay, skip):
+    rows = sum(p[0].shape[0] for p in projected)
+    x_cols, cols = projected[0][0].shape[1], taps.shape[1]
     requests, state_size, margin = table.shape[1] - 1, 128, 32
     return pl.pallas_call(
         inner_kernel,
-        out_shape=(
-            jax.ShapeDtypeStruct((x_cols // 128, rows + margin, 128), F32),
-            jax.ShapeDtypeStruct((rows + margin, 128), F32),
-            jax.ShapeDtypeStruct((rows + margin, 128), F32),
-        ),
-        in_specs=[SMEM] * 2 + [HBM] * 13 + [VMEM] * 8,
-        out_specs=(VMEM, VMEM, VMEM),
+        out_shape=jax.ShapeDtypeStruct((x_cols // 128 + 2, rows + margin, 128), F32),
+        in_specs=[SMEM] * 2 + [HBM] * 6 + [VMEM] * 10,
+        out_specs=VMEM,
         scratch_shapes=[
             pltpu.VMEM((rows + 8, cols), F32),
             pltpu.VMEM((rows + TILE, x_cols), BF16),
@@ -418,27 +414,24 @@
             pltpu.VMEM((rows, 128), BF16),
             pltpu.VMEM((rows + TILE, 128), F32),
             pltpu.VMEM((rows + TILE, 128), F32),
-        ]
-        + weight_scratch(weights, 3 * block_rows, len(blocks))
-        + [
             pltpu.VMEM((requests, state_size, x_cols), BF16),
             pltpu.SemaphoreType.DMA((requests,)),
             pltpu.VMEM((8 * PRIORS, x_cols), BF16),
             pltpu.SemaphoreType.DMA((2,)),
         ],
         compiler_params=pltpu.CompilerParams(vmem_limit_bytes=MOST),
-        cost_estimate=pl.CostEstimate(flops=16000000000, bytes_accessed=18000000, transcendentals=2000000),
+        cost_estimate=pl.CostEstimate(flops=14000000000, bytes_accessed=18000000, transcendentals=2000000),
         name="mixer_inner",
-    )(z, table, *blocks, *weights, *parts, *priors, *projected, info, columns, taps, bias, decay, skip)
-
-
-def mixer_late(table, first, arrays, c_rows, fade, total, rows):
-    x_cols = total.shape[0] * 128
-    state_size, requests = c_rows.shape[1], table.shape[1] - 1
+    )(z, table, *parts, *priors, *projected[0], *projected[1], info, columns, taps, bias, decay, skip)
+
+
+def mixer_late(table, first, arrays, total, rows):
+    x_cols = (total.shape[0] - 2) * 128
+    state_size, requests = total.shape[2], table.shape[1] - 1
     return pl.pallas_call(
         lambda *refs: late_kernel(first, len(arrays), *refs),
         out_shape=jax.ShapeDtypeStruct((rows, x_cols), BF16),
-        in_specs=[SMEM] + [HBM] * len(arrays) + [VMEM] * 2 + [HBM],
+        in_specs=[SMEM] + [ANY] * (len(arrays) + 1),
         out_specs=VMEM,
         scratch_shapes=[
             pltpu.VMEM((requests, state_size, x_cols), BF16),
@@ -446,10 +439,10 @@
             pltpu.SemaphoreType.DMA((requests,)),
             pltpu.SemaphoreType.DMA,
         ],
-        compiler_params=pltpu.CompilerParams(vmem_limit_bytes=MOST),
+        compiler_params=pltpu.CompilerParams(vmem_limit_bytes=24 * 1024 * 1024),
         cost_estimate=pl.CostEstimate(flops=500000000, bytes_accessed=13000000, transcendentals=0),
         name="mixer_late",
-    )(table, *arrays, c_rows, fade, total)
+    )(table, *arrays, total)
 
 
 def shards(
@@ -507,10 +500,10 @@
         jnp.repeat(skip_gain, head_size)[None],
     )
 
-    def inner(blocks, projected, parts, priors, tables):
-        table, weights, info, columns, taps, bias, decay, skip = tables
+    def inner(projected, parts, priors, tables):
+        table, _, info, columns, taps, bias, decay, skip = tables
         sums = mixer_inner(
-            z.reshape(1), table, blocks, weights, parts, priors, projected, info, columns, taps,
+            z.reshape(1), table, parts, priors, projected, info, columns, taps,
             bias, decay, skip,
         )
         return sums, table
@@ -520,8 +513,8 @@
     pool = jnp.concatenate(
         [states.reshape(slots * state_size, x_cols), conv_x_pool.reshape(slots * 3, x_cols), conv_bc]
     )
-    late, ((total, c_rows, fade), table) = gather(pool, tokens, tables, project, inner)
-    return mixer_late(table, 4, late, c_rows, fade, total, NZ * tokens.shape[0])
+    late, (total, table) = gather(pool, tokens, tables, project, inner)
+    return mixer_late(table, 4, late, total, NZ * tokens.shape[0])
 
 
 def solution(mesh):

time: 125 us -> 114 us (0.912); the launches traced: 123 us -> 114 us
  waiting for transfers between devices: 29.7 us -> 21.2 us
  starting transfers between devices: 34.2 us -> 31.8 us
  local copies, waits for them, and re-layouts: 11.7 us -> 14 us
    ppermute x16 -> x14, waiting for transfers between devices: 14.6 us -> 6.46 us  [on_cache(): return lax.ppermute(value, 'cache', pairs)]
    pallas_call x1, Pallas kernels: 21.7 us -> 14.9 us  [mixer_inner(): pl.pallas_call(inner_kernel, out_shape=jax.ShapeDtypeStruct((x_cols // 12...]
    pallas_call x1 -> x2, Pallas kernels: 7.89 us -> 14.2 us  [project(): pl.pallas_call(project_kernel, out_shape=(jax.ShapeDtypeStruct((rows, x_c...]
    ppermute x16 -> x14, starting transfers between devices: 20.9 us -> 16.7 us  [on_cache(): return lax.ppermute(value, 'cache', pairs)]
    unnamed x50 -> x46, local copies, waits for them, and re-layouts: 7.08 us -> 9.51 us
    ppermute x8, starting transfers between devices: 13.2 us -> 15.1 us  [over_z(): return lax.ppermute(value, 'tp', [(z, (z + step) % NZ) for z in range(NZ)])]
  transfers between devices with their start and end apart: 24 -> 22, of which waited for: 10 -> 7; matrix products, arithmetic and copies ran while one was open for 8% -> 9% of each run, Pallas kernels for 28% -> 32%
where the time goes in v1:
time: 114 us
  Pallas kernels  43.7 us (38%)
  starting transfers between devices  31.8 us (28%)
  waiting for transfers between devices  21.2 us (19%)
  local copies, waits for them, and re-layouts  14 us (12%)
  other arithmetic  2.79 us (2%)
    ppermute x14, starting transfers between devices, on_cache(): return lax.ppermute(value, 'cache', pairs)  16.7 us
    ppermute x8, starting transfers between devices, over_z(): return lax.ppermute(value, 'tp', [(z, (z + step) % NZ) for z in range(NZ)])  15.1 us
    pallas_call x1, Pallas kernels, mixer_inner(): pl.pallas_call(inner_kernel, out_shape=jax.ShapeDtypeStruct((x_cols // 12...  14.9 us
    ppermute x8, waiting for transfers between devices, over_z(): return lax.ppermute(value, 'tp', [(z, (z + step) % NZ) for z in range(NZ)])  14.7 us
    pallas_call x2, Pallas kernels, project(): pl.pallas_call(project_kernel, out_shape=(jax.ShapeDtypeStruct((rows, x_c...  14.2 us
    unnamed x46, local copies, waits for them, and re-layouts  9.51 us
    pallas_call x4, Pallas kernels, moved(): pl.pallas_call(kernel, out_shape=[jax.ShapeDtypeStruct(shape, sources[0]....  9.19 us
    ppermute x14, waiting for transfers between devices, on_cache(): return lax.ppermute(value, 'cache', pairs)  6.46 us
  transfers between devices with their start and end apart: 22, of which 7 were waited for; matrix products, arithmetic and copies ran while one was open for 9% of the time, Pallas kernels for 32%

profile of v1, /device:TPU:1, one launch (start us, length us, event | category | flops | bytes accessed | tf_op | source)
XLA Modules:
  0.0 113.9 jit_solution(8771801001093835658)
XLA Ops:
  0.0 2.5 %collective-permute-start.3 = (bf16[64,4096]{1,0:T(8,128)(2,1)}, bf16[64,4096]{1,0:T(8,128)(2,1)}, u32[]{:S(2)}, u32[]{:S(2)}) collective-permute-start(bf16[64,4096]{1,0:T(8,128)(2,1)} %refs_0_), channel_id=1, source_target_pairs={{0,1},{1,2},{2,3},{3,4},{4,5},{5,6},{6,7},{7,0},{8,9},{9,10},{10,1... | collective-permute-start | bytes 1572872 | tf_op jit(solution)/shard_map/ppermute | solution.py:37
  2.6 4.0 %collective-permute-start.5 = (bf16[64,4096]{1,0:T(8,128)(2,1)}, bf16[64,4096]{1,0:T(8,128)(2,1)}, u32[]{:S(2)}, u32[]{:S(2)}) collective-permute-start(bf16[64,4096]{1,0:T(8,128)(2,1)} %refs_0_), channel_id=1, source_target_pairs={{0,7},{1,0},{2,1},{3,2},{4,3},{5,4},{6,5},{7,6},{8,15},{9,8},{10,9... | collective-permute-start | bytes 1572872 | tf_op jit(solution)/shard_map/ppermute | solution.py:37
  8.0 1.2 %copy.27 = bf16[2,1024,128]{1,2,0:T(8,128)(2,1)S(1)} copy(bf16[2,1024,128]{2,1,0:T(8,128)(2,1)} %bitcast.70) | data formatting | bytes 1048576 | tf_op jit(solution)/shard_map/reshape | solution.py:511
  9.3 3.0 %collective-permute-start.2 = (bf16[272,1024]{1,0:T(8,128)(2,1)S(1)}, bf16[272,1024]{1,0:T(8,128)(2,1)S(1)}, u32[]{:S(2)}, u32[]{:S(2)}) collective-permute-start(bf16[272,1024]{1,0:T(8,128)(2,1)S(1)} %fusion.1.refs_0_), channel_id=1, source_target_pairs={{0,32},{8,136},{16,48},{24,152},{32,0},{40,168},{48,16},{56,184},{... | collective-permute-start | bytes 1671176 | tf_op jit(solution)/shard_map/ppermute | solution.py:41
  14.7 0.8 multiply_add_fusion
  15.7 0.8 iota_add_fusion.1
  17.4 1.6 %copy.36 = bf16[512,8,2,128]{3,1,2,0:T(8,128)(2,1)} copy(bf16[512,8,2,128]{3,2,1,0:T(2,128)(2,1)S(1)} %bitcast.66) | data formatting | bytes 4194304
  19.7 2.7 %collective-permute-start.6 = (bf16[64,4096]{1,0:T(8,128)(2,1)}, bf16[64,4096]{1,0:T(8,128)(2,1)S(1)}, u32[]{:S(2)}, u32[]{:S(2)}) collective-permute-start(bf16[64,4096]{1,0:T(8,128)(2,1)} %collective-permute-done.5.refs_2_), channel_id=1, source_target_pairs={{0,7},{1,0},{2,1},{3,2},{4,3},{5,4},{6,5},{7,6},{8,15},{9,8},{10,9... | collective-permute-start | bytes 1572872 | tf_op jit(solution)/shard_map/ppermute | solution.py:37
  23.5 2.5 %collective-permute-done.1.refs_2_ = bf16[272,1024]{1,0:T(8,128)(2,1)} collective-permute-done((bf16[272,1024]{1,0:T(8,128)(2,1)S(1)}, bf16[272,1024]{1,0:T(8,128)(2,1)}, u32[]{:S(2)}, u32[]{:S(2)}) %collective-permute-start.1) | collective-permute-done | bytes 557088 | tf_op jit(solution)/shard_map/ppermute | solution.py:41
  26.1 3.0 %lined.1 = (bf16[1088,1024]{1,0:T(8,128)(2,1)}, bf16[64,1024]{1,0:T(8,128)(2,1)}) custom-call(bf16[272,1024]{1,0:T(8,128)(2,1)} %copy-done.3, bf16[272,1024]{1,0:T(8,128)(2,1)} %collective-permute-done.refs_1_, bf16[272,1024]{1,0:T(8,128)(2,1)} %collective-permute-done.1.refs_2_, bf16[272,1024]{1,0:T(8,128)(2,1)} %copy-done.5), custom_call_target="tpu_custom_call" | custom-call | bytes 4000000 | tf_op jit(solution)/shard_map/lined/pallas_call | solution.py:62
  29.1 3.8 %collective-permute-done.4.refs_3_ = bf16[64,4096]{1,0:T(8,128)(2,1)S(1)} collective-permute-done((bf16[64,4096]{1,0:T(8,128)(2,1)}, bf16[64,4096]{1,0:T(8,128)(2,1)S(1)}, u32[]{:S(2)}, u32[]{:S(2)}) %collective-permute-start.4) | collective-permute-done | bytes 524320 | tf_op jit(solution)/shard_map/ppermute | solution.py:37
  32.9 0.8 copy-done.17
  33.7 2.6 %collective-permute-start.14 = (bf16[1088,1024]{1,0:T(8,128)(2,1)}, bf16[1088,1024]{1,0:T(8,128)(2,1)}, u32[]{:S(2)}, u32[]{:S(2)}) collective-permute-start(bf16[1088,1024]{1,0:T(8,128)(2,1)} %get-tuple-element.62.s0), channel_id=1, source_target_pairs={{0,8},{8,0},{16,24},{24,16},{32,40},{40,32},{48,56},{56,48},{64,72... | collective-permute-start | bytes 6684680 | tf_op jit(solution)/shard_map/ppermute | solution.py:41
  36.3 2.5 %collective-permute-start.8 = (bf16[1088,1024]{1,0:T(8,128)(2,1)}, bf16[1088,1024]{1,0:T(8,128)(2,1)S(1)}, u32[]{:S(2)}, u32[]{:S(2)}) collective-permute-start(bf16[1088,1024]{1,0:T(8,128)(2,1)} %get-tuple-element.62.s0), channel_id=1, source_target_pairs={{0,192},{8,56},{16,208},{24,8},{32,224},{40,24},{48,240},{56,40},{... | collective-permute-start | bytes 6684680 | tf_op jit(solution)/shard_map/ppermute | solution.py:41
  38.8 2.9 %collective-permute-start.11 = (bf16[64,4096]{1,0:T(8,128)(2,1)}, bf16[64,4096]{1,0:T(8,128)(2,1)S(1)}, u32[]{:S(2)}, u32[]{:S(2)}) collective-permute-start(bf16[64,4096]{1,0:T(8,128)(2,1)} %copy-done.17), channel_id=1, source_target_pairs={{0,7},{1,0},{2,1},{3,2},{4,3},{5,4},{6,5},{7,6},{8,15},{9,8},{10,9... | collective-permute-start | bytes 1572872 | tf_op jit(solution)/shard_map/ppermute | solution.py:37
  41.7 7.9 %project.2 = (bf16[320,1024]{1,0:T(8,128)(2,1)}, bf16[320,384]{1,0:T(8,128)(2,1)}) custom-call(bf16[64,4096]{1,0:T(8,128)(2,1)} %refs_0_, bf16[64,4096]{1,0:T(8,128)(2,1)} %collective-permute-done.3.refs_1_, bf16[64,4096]{1,0:T(8,128)(2,1)} %collective-permute-done.5.refs_2_, bf16[64,4096]{1,0:T(8,128)(2,1)} %copy-done.16, bf16[64,4096]{1,0:T(8,128)(2,1)} %copy-done.17, ...), custom_call_target="tpu_custom_call" | custom-call | flops 8000000000 | bytes 14000000 | tf_op jit(solution)/shard_map/project/pallas_call | solution.py:386
  49.5 4.4 %collective-permute-done.10.refs_0_ = bf16[64,4096]{1,0:T(8,128)(2,1)S(1)} collective-permute-done((bf16[64,4096]{1,0:T(8,128)(2,1)}, bf16[64,4096]{1,0:T(8,128)(2,1)S(1)}, u32[]{:S(2)}, u32[]{:S(2)}) %collective-permute-start.10) | collective-permute-done | bytes 524320 | tf_op jit(solution)/shard_map/ppermute | solution.py:37
  54.9 1.8 %halves.2 = (bf16[32,4096]{1,0:T(8,128)(2,1)}, bf16[32,4096]{1,0:T(8,128)(2,1)}) custom-call(bf16[64,4096]{1,0:T(8,128)(2,1)} %copy-done.6, bf16[64,4096]{1,0:T(8,128)(2,1)} %copy-done.7), custom_call_target="tpu_custom_call" | custom-call | bytes 4000000 | tf_op jit(solution)/shard_map/halves/pallas_call | solution.py:62
  56.7 2.0 %collective-permute-start.12 = (bf16[32,4096]{1,0:T(8,128)(2,1)}, bf16[32,4096]{1,0:T(8,128)(2,1)S(1)}, u32[]{:S(2)}, u32[]{:S(2)}) collective-permute-start(bf16[32,4096]{1,0:T(8,128)(2,1)} %get-tuple-element.80), channel_id=1, source_target_pairs={{0,1},{1,2},{2,3},{3,4},{4,5},{5,6},{6,7},{7,0},{8,9},{9,10},{10,1... | collective-permute-start | bytes 786440 | tf_op jit(solution)/shard_map/ppermute | solution.py:37
  58.7 0.9 collective-permute-start.13
  59.6 6.1 %collective-permute-done.12.refs_2_ = bf16[32,4096]{1,0:T(8,128)(2,1)S(1)} collective-permute-done((bf16[32,4096]{1,0:T(8,128)(2,1)}, bf16[32,4096]{1,0:T(8,128)(2,1)S(1)}, u32[]{:S(2)}, u32[]{:S(2)}) %collective-permute-start.12) | collective-permute-done | bytes 262176 | tf_op jit(solution)/shard_map/ppermute | solution.py:37
  66.7 6.4 %project.3 = (bf16[192,1024]{1,0:T(8,128)(2,1)}, bf16[192,384]{1,0:T(8,128)(2,1)}) custom-call(bf16[64,4096]{1,0:T(8,128)(2,1)} %copy-done.6, bf16[64,4096]{1,0:T(8,128)(2,1)} %copy-done.7, bf16[32,4096]{1,0:T(8,128)(2,1)} %copy-done.19, bf16[32,4096]{1,0:T(8,128)(2,1)} %copy-done.20, bf16[4096,1024]{1,0:T(8,128)(2,1)} %refs_4_, bf16[4096,256]{1,0:T(8,128)(2,1)} %bitcast.68, ...), custom_call_target="tpu_custom_call" | custom-call | flops 8000000000 | bytes 14000000 | tf_op jit(solution)/shard_map/project/pallas_call | solution.py:386
  74.5 1.8 %gathered_priors.1.p0 = bf16[256,1024]{1,0:T(8,128)(2,1)} custom-call(bf16[64,1024]{1,0:T(8,128)(2,1)} %get-tuple-element.63.refs_0_, bf16[1088,1024]{1,0:T(8,128)(2,1)} %collective-permute-done.7.refs_0_.refs_1_.s2, bf16[1088,1024]{1,0:T(8,128)(2,1)} %copy-done.2, bf16[64,1024]{1,0:T(8,128)(2,1)} %copy-done.9), custom_call_target="tpu_custom_call" | custom-call | bytes 4000000 | tf_op jit(solution)/shard_map/gathered_priors/pallas_call | solution.py:62
  76.3 3.2 %collective-permute-start.17 = (bf16[256,1024]{1,0:T(8,128)(2,1)}, bf16[256,1024]{1,0:T(8,128)(2,1)S(1)}, u32[]{:S(2)}, u32[]{:S(2)}) collective-permute-start(bf16[256,1024]{1,0:T(8,128)(2,1)} %gathered_priors.1.p0), channel_id=1, source_target_pairs={{0,8},{8,0},{16,24},{24,16},{32,40},{40,32},{48,56},{56,48},{64,72... | collective-permute-start | bytes 1572872 | tf_op jit(solution)/shard_map/ppermute | solution.py:41
  80.2 2.6 %halves.3 = (bf16[512,1024]{1,0:T(8,128)(2,1)}, bf16[512,1024]{1,0:T(8,128)(2,1)}) custom-call(bf16[1088,1024]{1,0:T(8,128)(2,1)} %collective-permute-done.7.refs_0_.refs_1_.s2, bf16[1088,1024]{1,0:T(8,128)(2,1)} %copy-done.2), custom_call_target="tpu_custom_call" | custom-call | bytes 4000000 | tf_op jit(solution)/shard_map/halves/pallas_call | solution.py:62
  83.8 2.3 %collective-permute-start.16 = (bf16[512,1024]{1,0:T(8,128)(2,1)}, bf16[512,1024]{1,0:T(8,128)(2,1)}, u32[]{:S(2)}, u32[]{:S(2)}) collective-permute-start(bf16[512,1024]{1,0:T(8,128)(2,1)} %get-tuple-element.91), channel_id=1, source_target_pairs={{0,192},{8,56},{16,208},{24,8},{32,224},{40,24},{48,240},{56,40},{... | collective-permute-start | bytes 3145736 | tf_op jit(solution)/shard_map/ppermute | solution.py:41
  86.1 0.8 copy-done.18
  86.9 14.9 %mixer_inner.1.refs_7_ = f32[10,544,128]{2,1,0:T(8,128)} custom-call(s32[1]{0:T(128)} %bitcast.13.where, s32[4,33]{1,0:T(4,128)} %pad.21.table.refs_0_, bf16[1088,1024]{1,0:T(8,128)(2,1)} %get-tuple-element.62.s0, bf16[1088,1024]{1,0:T(8,128)(2,1)} %collective-permute-done.14.s1, bf16[1088,1024]{1,0:T(8,128)(2,1)} %collective-permute-done.7.refs_0_.refs_1_.s2, ...), custom_call_target="tpu_custom_call" | custom-call | flops 14000000000 | bytes 18000000 | tf_op jit(solution)/shard_map/mixer_inner/pallas_call | solution.py:405
  102.6 2.7 %collective-permute-done.20.refs_4_ = bf16[512,1024]{1,0:T(8,128)(2,1)S(1)} collective-permute-done((bf16[512,1024]{1,0:T(8,128)(2,1)S(1)}, bf16[512,1024]{1,0:T(8,128)(2,1)S(1)}, u32[]{:S(2)}, u32[]{:S(2)}) %collective-permute-start.20) | collective-permute-done | bytes 1048608 | tf_op jit(solution)/shard_map/ppermute | solution.py:41
  105.3 1.2 %collective-permute-done.21.refs_6_ = bf16[512,1024]{1,0:T(8,128)(2,1)S(1)} collective-permute-done((bf16[512,1024]{1,0:T(8,128)(2,1)}, bf16[512,1024]{1,0:T(8,128)(2,1)S(1)}, u32[]{:S(2)}, u32[]{:S(2)}) %collective-permute-start.21) | collective-permute-done | bytes 1048608 | tf_op jit(solution)/shard_map/ppermute | solution.py:41
  106.5 1.8 %copy-done = f32[10,544,128]{2,1,0:T(8,128)S(1)} copy-done((f32[10,544,128]{2,1,0:T(8,128)S(1)}, f32[10,544,128]{2,1,0:T(8,128)}, u32[]{:S(2)}) %copy-start) | copy-done | bytes 2785304
  108.3 5.4 %mixer_late.1 = bf16[512,1024]{1,0:T(8,128)(2,1)} custom-call(s32[4,33]{1,0:T(4,128)S(1)} %copy-done.1, bf16[1088,1024]{1,0:T(8,128)(2,1)S(1)} %collective-permute-done.18.refs_1_, bf16[1088,1024]{1,0:T(8,128)(2,1)} %collective-permute-done.19.refs_2_, bf16[512,1024]{1,0:T(8,128)(2,1)S(1)} %collective-permute-done.15.refs_3_, ...), custom_call_target="tpu_custom_call" | custom-call | flops 500000000 | bytes 13000000 | tf_op jit(solution)/shard_map/mixer_late/pallas_call | solution.py:431
  (91 shorter events, 12.5 us)
Async XLA Ops:
  0.0 13.8 %copy-start.13 = (s32[1,32]{1,0:T(1,128)S(1)}, s32[1,32]{1,0:T(1,128)}, u32[]{:S(2)}) copy-start(s32[1,32]{1,0:T(1,128)} %param.29) | copy-start | bytes 388
  0.0 13.9 %copy-start.11 = (bf16[4,2,128]{2,1,0:T(2,128)(2,1)S(1)}, bf16[4,2,128]{2,1,0:T(2,128)(2,1)}, u32[]{:S(2)}) copy-start(bf16[4,2,128]{2,1,0:T(2,128)(2,1)} %param.20) | copy-start | bytes 6148
  0.0 13.9 %copy-start.12 = (f32[16]{0:T(128)S(1)}, f32[16]{0:T(128)}, u32[]{:S(2)}) copy-start(f32[16]{0:T(128)} %param.23) | copy-start | bytes 196
  0.0 17.4 %copy-start.4 = (bf16[4096,2,128]{2,1,0:T(2,128)(2,1)S(1)}, bf16[4096,2,128]{2,1,0:T(2,128)(2,1)}, u32[]{:S(2)}) copy-start(bf16[4096,2,128]{2,1,0:T(2,128)(2,1)} %param.17) | copy-start | bytes 6291460
  0.0 19.6 %collective-permute-start.3 = (bf16[64,4096]{1,0:T(8,128)(2,1)}, bf16[64,4096]{1,0:T(8,128)(2,1)}, u32[]{:S(2)}, u32[]{:S(2)}) collective-permute-start(bf16[64,4096]{1,0:T(8,128)(2,1)} %refs_0_), channel_id=1, source_target_pairs={{0,1},{1,2},{2,3},{3,4},{4,5},{5,6},{6,7},{7,0},{8,9},{9,10},{10,1... | collective-permute-start | bytes 1572872 | tf_op jit(solution)/shard_map/ppermute | solution.py:37
  2.6 17.1 %collective-permute-start.5 = (bf16[64,4096]{1,0:T(8,128)(2,1)}, bf16[64,4096]{1,0:T(8,128)(2,1)}, u32[]{:S(2)}, u32[]{:S(2)}) collective-permute-start(bf16[64,4096]{1,0:T(8,128)(2,1)} %refs_0_), channel_id=1, source_target_pairs={{0,7},{1,0},{2,1},{3,2},{4,3},{5,4},{6,5},{7,6},{8,15},{9,8},{10,9... | collective-permute-start | bytes 1572872 | tf_op jit(solution)/shard_map/ppermute | solution.py:37
  9.3 9.7 %copy-start.3 = (bf16[272,1024]{1,0:T(8,128)(2,1)}, bf16[272,1024]{1,0:T(8,128)(2,1)S(1)}, u32[]{:S(2)}) copy-start(bf16[272,1024]{1,0:T(8,128)(2,1)S(1)} %fusion.1.refs_0_) | copy-start | bytes 1671172
  9.3 14.2 %collective-permute-start.2 = (bf16[272,1024]{1,0:T(8,128)(2,1)S(1)}, bf16[272,1024]{1,0:T(8,128)(2,1)S(1)}, u32[]{:S(2)}, u32[]{:S(2)}) collective-permute-start(bf16[272,1024]{1,0:T(8,128)(2,1)S(1)} %fusion.1.refs_0_), channel_id=1, source_target_pairs={{0,32},{8,136},{16,48},{24,152},{32,0},{40,168},{48,16},{56,184},{... | collective-permute-start | bytes 1671176 | tf_op jit(solution)/shard_map/ppermute | solution.py:41
  12.3 13.7 %collective-permute-start.1 = (bf16[272,1024]{1,0:T(8,128)(2,1)S(1)}, bf16[272,1024]{1,0:T(8,128)(2,1)}, u32[]{:S(2)}, u32[]{:S(2)}) collective-permute-start(bf16[272,1024]{1,0:T(8,128)(2,1)S(1)} %fusion.1.refs_0_), channel_id=1, source_target_pairs={{0,48},{8,200},{16,0},{24,216},{32,16},{40,232},{48,32},{56,248},{... | collective-permute-start | bytes 1671176 | tf_op jit(solution)/shard_map/ppermute | solution.py:41
  13.1 13.0 %collective-permute-start = (bf16[272,1024]{1,0:T(8,128)(2,1)S(1)}, bf16[272,1024]{1,0:T(8,128)(2,1)}, u32[]{:S(2)}, u32[]{:S(2)}) collective-permute-start(bf16[272,1024]{1,0:T(8,128)(2,1)S(1)} %fusion.1.refs_0_), channel_id=1, source_target_pairs={{0,16},{8,72},{16,32},{24,88},{32,48},{40,104},{48,0},{56,120},{64... | collective-permute-start | bytes 1671176 | tf_op jit(solution)/shard_map/ppermute | solution.py:41
  17.4 5.0 %copy-start.15 = (f32[16]{0:T(128)S(1)}, f32[16]{0:T(128)}, u32[]{:S(2)}) copy-start(f32[16]{0:T(128)} %param.21) | copy-start | bytes 196
  17.4 5.5 %copy-start.10 = (bf16[4,1024]{1,0:T(4,128)(2,1)S(1)}, bf16[4,1024]{1,0:T(4,128)(2,1)}, u32[]{:S(2)}) copy-start(bf16[4,1024]{1,0:T(4,128)(2,1)} %param.19) | copy-start | bytes 24580
  19.6 13.3 %collective-permute-start.4 = (bf16[64,4096]{1,0:T(8,128)(2,1)}, bf16[64,4096]{1,0:T(8,128)(2,1)S(1)}, u32[]{:S(2)}, u32[]{:S(2)}) collective-permute-start(bf16[64,4096]{1,0:T(8,128)(2,1)} %collective-permute-done.3.refs_1_), channel_id=1, source_target_pairs={{0,1},{1,2},{2,3},{3,4},{4,5},{5,6},{6,7},{7,0},{8,9},{9,10},{10,1... | collective-permute-start | bytes 1572872 | tf_op jit(solution)/shard_map/ppermute | solution.py:37
  19.7 13.2 %collective-permute-start.6 = (bf16[64,4096]{1,0:T(8,128)(2,1)}, bf16[64,4096]{1,0:T(8,128)(2,1)S(1)}, u32[]{:S(2)}, u32[]{:S(2)}) collective-permute-start(bf16[64,4096]{1,0:T(8,128)(2,1)} %collective-permute-done.5.refs_2_), channel_id=1, source_target_pairs={{0,7},{1,0},{2,1},{3,2},{4,3},{5,4},{6,5},{7,6},{8,15},{9,8},{10,9... | collective-permute-start | bytes 1572872 | tf_op jit(solution)/shard_map/ppermute | solution.py:37
  32.9 5.9 %copy-start.16 = (bf16[64,4096]{1,0:T(8,128)(2,1)}, bf16[64,4096]{1,0:T(8,128)(2,1)S(1)}, u32[]{:S(2)}) copy-start(bf16[64,4096]{1,0:T(8,128)(2,1)S(1)} %collective-permute-done.4.refs_3_) | copy-start | bytes 1572868
  33.7 32.0 %copy-start.8 = (bf16[64,1024]{1,0:T(8,128)(2,1)S(1)}, bf16[64,1024]{1,0:T(8,128)(2,1)}, u32[]{:S(2)}) copy-start(bf16[64,1024]{1,0:T(8,128)(2,1)} %get-tuple-element.63.refs_0_) | copy-start | bytes 393220
  33.7 32.3 %collective-permute-start.14 = (bf16[1088,1024]{1,0:T(8,128)(2,1)}, bf16[1088,1024]{1,0:T(8,128)(2,1)}, u32[]{:S(2)}, u32[]{:S(2)}) collective-permute-start(bf16[1088,1024]{1,0:T(8,128)(2,1)} %get-tuple-element.62.s0), channel_id=1, source_target_pairs={{0,8},{8,0},{16,24},{24,16},{32,40},{40,32},{48,56},{56,48},{64,72... | collective-permute-start | bytes 6684680 | tf_op jit(solution)/shard_map/ppermute | solution.py:41
  36.3 36.9 %collective-permute-start.8 = (bf16[1088,1024]{1,0:T(8,128)(2,1)}, bf16[1088,1024]{1,0:T(8,128)(2,1)S(1)}, u32[]{:S(2)}, u32[]{:S(2)}) collective-permute-start(bf16[1088,1024]{1,0:T(8,128)(2,1)} %get-tuple-element.62.s0), channel_id=1, source_target_pairs={{0,192},{8,56},{16,208},{24,8},{32,224},{40,24},{48,240},{56,40},{... | collective-permute-start | bytes 6684680 | tf_op jit(solution)/shard_map/ppermute | solution.py:41
  38.7 34.4 %collective-permute-start.7 = (bf16[1088,1024]{1,0:T(8,128)(2,1)}, bf16[1088,1024]{1,0:T(8,128)(2,1)}, u32[]{:S(2)}, u32[]{:S(2)}) collective-permute-start(bf16[1088,1024]{1,0:T(8,128)(2,1)} %get-tuple-element.62.s0), channel_id=1, source_target_pairs={{0,64},{8,24},{16,80},{24,40},{32,96},{40,56},{48,112},{56,8},{64,... | collective-permute-start | bytes 6684680 | tf_op jit(solution)/shard_map/ppermute | solution.py:41
  38.8 15.2 %collective-permute-start.10 = (bf16[64,4096]{1,0:T(8,128)(2,1)}, bf16[64,4096]{1,0:T(8,128)(2,1)S(1)}, u32[]{:S(2)}, u32[]{:S(2)}) collective-permute-start(bf16[64,4096]{1,0:T(8,128)(2,1)} %copy-done.16), channel_id=1, source_target_pairs={{0,1},{1,2},{2,3},{3,4},{4,5},{5,6},{6,7},{7,0},{8,9},{9,10},{10,1... | collective-permute-start | bytes 1572872 | tf_op jit(solution)/shard_map/ppermute | solution.py:37
  38.8 15.2 %collective-permute-start.11 = (bf16[64,4096]{1,0:T(8,128)(2,1)}, bf16[64,4096]{1,0:T(8,128)(2,1)S(1)}, u32[]{:S(2)}, u32[]{:S(2)}) collective-permute-start(bf16[64,4096]{1,0:T(8,128)(2,1)} %copy-done.17), channel_id=1, source_target_pairs={{0,7},{1,0},{2,1},{3,2},{4,3},{5,4},{6,5},{7,6},{8,15},{9,8},{10,9... | collective-permute-start | bytes 1572872 | tf_op jit(solution)/shard_map/ppermute | solution.py:37
  56.7 9.0 %collective-permute-start.12 = (bf16[32,4096]{1,0:T(8,128)(2,1)}, bf16[32,4096]{1,0:T(8,128)(2,1)S(1)}, u32[]{:S(2)}, u32[]{:S(2)}) collective-permute-start(bf16[32,4096]{1,0:T(8,128)(2,1)} %get-tuple-element.80), channel_id=1, source_target_pairs={{0,1},{1,2},{2,3},{3,4},{4,5},{5,6},{6,7},{7,0},{8,9},{9,10},{10,1... | collective-permute-start | bytes 786440 | tf_op jit(solution)/shard_map/ppermute | solution.py:37
  58.7 7.3 %collective-permute-start.13 = (bf16[32,4096]{1,0:T(8,128)(2,1)}, bf16[32,4096]{1,0:T(8,128)(2,1)S(1)}, u32[]{:S(2)}, u32[]{:S(2)}) collective-permute-start(bf16[32,4096]{1,0:T(8,128)(2,1)} %get-tuple-element.81), channel_id=1, source_target_pairs={{0,7},{1,0},{2,1},{3,2},{4,3},{5,4},{6,5},{7,6},{8,15},{9,8},{10,9... | collective-permute-start | bytes 786440 | tf_op jit(solution)/shard_map/ppermute | solution.py:37
  65.7 7.4 %collective-permute-start.9 = (bf16[64,1024]{1,0:T(8,128)(2,1)S(1)}, bf16[64,1024]{1,0:T(8,128)(2,1)S(1)}, u32[]{:S(2)}, u32[]{:S(2)}) collective-permute-start(bf16[64,1024]{1,0:T(8,128)(2,1)S(1)} %copy-done.8), channel_id=1, source_target_pairs={{0,128},{8,40},{16,144},{24,56},{32,160},{40,8},{48,176},{56,24},{... | collective-permute-start | bytes 393224 | tf_op jit(solution)/shard_map/ppermute | solution.py:41
  76.3 9.8 %collective-permute-start.17 = (bf16[256,1024]{1,0:T(8,128)(2,1)}, bf16[256,1024]{1,0:T(8,128)(2,1)S(1)}, u32[]{:S(2)}, u32[]{:S(2)}) collective-permute-start(bf16[256,1024]{1,0:T(8,128)(2,1)} %gathered_priors.1.p0), channel_id=1, source_target_pairs={{0,8},{8,0},{16,24},{24,16},{32,40},{40,32},{48,56},{56,48},{64,72... | collective-permute-start | bytes 1572872 | tf_op jit(solution)/shard_map/ppermute | solution.py:41
  82.9 23.6 %collective-permute-start.18 = (bf16[1088,1024]{1,0:T(8,128)(2,1)}, bf16[1088,1024]{1,0:T(8,128)(2,1)S(1)}, u32[]{:S(2)}, u32[]{:S(2)}) collective-permute-start(bf16[1088,1024]{1,0:T(8,128)(2,1)} %collective-permute-done.7.refs_0_.refs_1_.s2), channel_id=1, source_target_pairs={{0,8},{8,0},{16,24},{24,16},{32,40},{40,32},{48,56},{56,48},{64,72... | collective-permute-start | bytes 6684680 | tf_op jit(solution)/shard_map/ppermute | solution.py:41
  83.0 23.5 %collective-permute-start.19 = (bf16[1088,1024]{1,0:T(8,128)(2,1)}, bf16[1088,1024]{1,0:T(8,128)(2,1)}, u32[]{:S(2)}, u32[]{:S(2)}) collective-permute-start(bf16[1088,1024]{1,0:T(8,128)(2,1)} %copy-done.2), channel_id=1, source_target_pairs={{0,8},{8,0},{16,24},{24,16},{32,40},{40,32},{48,56},{56,48},{64,72... | collective-permute-start | bytes 6684680 | tf_op jit(solution)/shard_map/ppermute | solution.py:41
  83.5 18.4 %collective-permute-start.15 = (bf16[512,1024]{1,0:T(8,128)(2,1)}, bf16[512,1024]{1,0:T(8,128)(2,1)S(1)}, u32[]{:S(2)}, u32[]{:S(2)}) collective-permute-start(bf16[512,1024]{1,0:T(8,128)(2,1)} %get-tuple-element.90), channel_id=1, source_target_pairs={{0,64},{8,24},{16,80},{24,40},{32,96},{40,56},{48,112},{56,8},{64,... | collective-permute-start | bytes 3145736 | tf_op jit(solution)/shard_map/ppermute | solution.py:41
  83.8 18.0 %collective-permute-start.16 = (bf16[512,1024]{1,0:T(8,128)(2,1)}, bf16[512,1024]{1,0:T(8,128)(2,1)}, u32[]{:S(2)}, u32[]{:S(2)}) collective-permute-start(bf16[512,1024]{1,0:T(8,128)(2,1)} %get-tuple-element.91), channel_id=1, source_target_pairs={{0,192},{8,56},{16,208},{24,8},{32,224},{40,24},{48,240},{56,40},{... | collective-permute-start | bytes 3145736 | tf_op jit(solution)/shard_map/ppermute | solution.py:41
  86.9 19.6 %copy-start.1 = (s32[4,33]{1,0:T(4,128)S(1)}, s32[4,33]{1,0:T(4,128)}, u32[]{:S(2)}) copy-start(s32[4,33]{1,0:T(4,128)} %pad.21.table.refs_0_) | copy-start | bytes 1588
  101.8 3.4 %collective-permute-start.20 = (bf16[512,1024]{1,0:T(8,128)(2,1)S(1)}, bf16[512,1024]{1,0:T(8,128)(2,1)S(1)}, u32[]{:S(2)}, u32[]{:S(2)}) collective-permute-start(bf16[512,1024]{1,0:T(8,128)(2,1)S(1)} %collective-permute-done.15.refs_3_), channel_id=1, source_target_pairs={{0,8},{8,0},{16,24},{24,16},{32,40},{40,32},{48,56},{56,48},{64,72... | collective-permute-start | bytes 3145736 | tf_op jit(solution)/shard_map/ppermute | solution.py:41
  102.5 4.0 %collective-permute-start.21 = (bf16[512,1024]{1,0:T(8,128)(2,1)}, bf16[512,1024]{1,0:T(8,128)(2,1)S(1)}, u32[]{:S(2)}, u32[]{:S(2)}) collective-permute-start(bf16[512,1024]{1,0:T(8,128)(2,1)} %collective-permute-done.16.refs_5_), channel_id=1, source_target_pairs={{0,8},{8,0},{16,24},{24,16},{32,40},{40,32},{48,56},{56,48},{64,72... | collective-permute-start | bytes 3145736 | tf_op jit(solution)/shard_map/ppermute | solution.py:41
  (11 other events, 16.1 us)

commit v2 on v1

--- a/solution.py
+++ b/solution.py
@@ -109,20 +109,22 @@
 
     near_up, near_down = on_cache(line, second_round(1)), on_cache(line, second_round(-1))
     far_prior = on_cache(line_prior, second_round(2))
-    line_other = on_cache(line, CORES)
-    projected = [project(blocks, tables[1])]
+    to_send, far_prior = tie((line, far_prior))
+    line_other = on_cache(to_send, CORES)
+    projected = [project(blocks, tables[1], 24000000000)]
     up, down = over_z(up, 1), over_z(down, -1)
     up, down, projected = tie((up, down, projected))
     last_up, last_down = halves(up, down)
     blocks = [up, down, over_z(last_up, 1), over_z(last_down, -1)]
-    blocks, line_other = tie((blocks, line_other))
-    projected.append(project(blocks, tables[1]))
-    near_up, near_down, far_prior, projected = tie((near_up, near_down, far_prior, projected))
+    near_up, near_down, far_prior, up, down = tie((near_up, near_down, far_prior, up, down))
 
     priors = gathered_priors([line_prior, near_up, near_down, far_prior])
-    priors = [priors, on_cache(priors, CORES)]
     far_up, far_down = halves(near_up, near_down, PRIORS)
     far_up, far_down = on_cache(far_up, second_round(1)), on_cache(far_down, second_round(-1))
+    priors = [priors, on_cache(priors, CORES)]
+    blocks, line_other = tie((blocks, line_other))
+    projected.append(project(blocks, tables[1], 24000000000))
+    near_up, near_down, projected = tie((near_up, near_down, projected))
     up_other, down_other = on_cache(near_up, CORES), on_cache(near_down, CORES)
     result = inner(projected, [line, line_other, near_up, near_down], priors, tables)
     far_up, far_down, result = tie((far_up, far_down, result))
@@ -176,6 +178,7 @@
     raw, xs, bs, cs, run, step, states, state_sem, prior, prior_sem,
 ):
     rows = raw.shape[0] - 8
+    columns = cols_in[...].T
     x_cols = xs.shape[1]
     c_ref, fade_ref = sum_ref.at[x_cols // 128], sum_ref.at[x_cols // 128 + 1]
     cols = taps.shape[1]
@@ -211,17 +214,17 @@
 
     def requests_at(first, count):
         spot = first + lax.broadcasted_iota(jnp.int32, (info.shape[1], count), 1)
-        found = jnp.sum(jnp.where(spot >= cols_in[:, 1:2], 1.0, 0.0), axis=0, keepdims=True)
+        found = jnp.sum(jnp.where(spot.astype(F32) >= columns[:, 1:2], 1.0, 0.0), axis=0, keepdims=True)
         return jnp.where(spot[0:1] < 0, -1.0, found)
 
     before = lax.broadcasted_iota(jnp.int32, (rows, rows), 0) >= lax.broadcasted_iota(
         jnp.int32, (rows, rows), 1
     )
     sums = jnp.where((req_col == requests_at(0, rows)) & before, 1.0, 0.0).astype(BF16)
-    slot_ids = lax.broadcasted_iota(jnp.int32, (cols_in.shape[0], prior.shape[0]), 1)
-    pick_x = jnp.where(slot_ids == cols_in[:, 0:1], 1.0, 0.0).astype(BF16)
-    pick_bc = jnp.where(slot_ids == cols_in[:, 0:1] + 6, 1.0, 0.0).astype(BF16)
-    spot_ids = lax.broadcasted_iota(jnp.int32, (rows, cols_in.shape[0]), 1).astype(F32)
+    slot_ids = lax.broadcasted_iota(jnp.int32, (columns.shape[0], prior.shape[0]), 1).astype(F32)
+    pick_x = jnp.where(slot_ids == columns[:, 0:1], 1.0, 0.0).astype(BF16)
+    pick_bc = jnp.where(slot_ids == columns[:, 0:1] + 6, 1.0, 0.0).astype(BF16)
+    spot_ids = lax.broadcasted_iota(jnp.int32, (rows, columns.shape[0]), 1).astype(F32)
     chosen = [
         jnp.where((spot_ids == 3 * req_col + offset + (3 - lag)) & (offset < lag), 1.0, 0.0).astype(BF16)
         for lag in (1, 2, 3)
@@ -381,7 +384,7 @@
     ]
 
 
-def project(blocks, weights):
+def project(blocks, weights, flops):
     rows, x_cols = sum(b.shape[0] for b in blocks), weights[0].shape[1]
     return pl.pallas_call(
         project_kernel,
@@ -393,7 +396,7 @@
         out_specs=(VMEM, VMEM),
         scratch_shapes=weight_scratch(weights, rows, len(blocks)),
         compiler_params=pltpu.CompilerParams(vmem_limit_bytes=MOST),
-        cost_estimate=pl.CostEstimate(flops=8000000000, bytes_accessed=14000000, transcendentals=0),
+        cost_estimate=pl.CostEstimate(flops=flops, bytes_accessed=14000000, transcendentals=0),
         name="project",
     )(*blocks, *weights)
 
@@ -494,7 +497,7 @@
     pad = (0, 128 - heads)
     from_row = (prior_row[:, None] + jnp.arange(3)[None, :]).reshape(-1)
     from_row = jnp.pad(from_row, (0, 128 - 3 * requests), constant_values=-16)
-    columns = jnp.stack([from_row, info[0]], axis=1)
+    columns = jnp.pad(jnp.stack([from_row, info[0]]).astype(F32), ((0, 6), (0, 0)))
     tables = (
         table, weights, info, columns, taps, jnp.pad(dt_bias, pad)[None], jnp.pad(decay_rate, pad)[None],
         jnp.repeat(skip_gain, head_size)[None],

time: 114 us -> 111 us (0.974)
  local copies, waits for them, and re-layouts: 14 us -> 12 us
  waiting for transfers between devices: 21.2 us -> 19.2 us
    ppermute x8, waiting for transfers between devices: 14.7 us -> 6.99 us  [over_z(): return lax.ppermute(value, 'tp', [(z, (z + step) % NZ) for z in range(NZ)])]
    ppermute x14, waiting for transfers between devices: 6.46 us -> 12.2 us  [on_cache(): return lax.ppermute(value, 'cache', pairs)]
    unnamed x46 -> x42, local copies, waits for them, and re-layouts: 9.51 us -> 7.51 us
  transfers between devices with their start and end apart: 22 -> 22, of which waited for: 7 -> 7; matrix products, arithmetic and copies ran while one was open for 9% -> 9% of each run, Pallas kernels for 32% -> 35%
where the time goes in v2:
time: 111 us; the launch traced here: 110 us
  Pallas kernels  43.4 us (39%)
  starting transfers between devices  32.5 us (29%)
  waiting for transfers between devices  19.2 us (17%)
  local copies, waits for them, and re-layouts  12 us (11%)
  other arithmetic  2.78 us (3%)
    ppermute x14, starting transfers between devices, on_cache(): return lax.ppermute(value, 'cache', pairs)  17.8 us
    pallas_call x1, Pallas kernels, mixer_inner(): pl.pallas_call(inner_kernel, out_shape=jax.ShapeDtypeStruct((x_cols // 12...  14.9 us
    ppermute x8, starting transfers between devices, over_z(): return lax.ppermute(value, 'tp', [(z, (z + step) % NZ) for z in range(NZ)])  14.7 us
    pallas_call x2, Pallas kernels, project(): pl.pallas_call(project_kernel, out_shape=(jax.ShapeDtypeStruct((rows, x_c...  14.2 us
    ppermute x14, waiting for transfers between devices, on_cache(): return lax.ppermute(value, 'cache', pairs)  12.2 us
    pallas_call x4, Pallas kernels, moved(): pl.pallas_call(kernel, out_shape=[jax.ShapeDtypeStruct(shape, sources[0]....  9.22 us
    unnamed x42, local copies, waits for them, and re-layouts  7.51 us
    ppermute x8, waiting for transfers between devices, over_z(): return lax.ppermute(value, 'tp', [(z, (z + step) % NZ) for z in range(NZ)])  6.99 us
  transfers between devices with their start and end apart: 22, of which 7 were waited for; matrix products, arithmetic and copies ran while one was open for 9% of the time, Pallas kernels for 35%

profile of v2, /device:TPU:1, one launch (start us, length us, event | category | flops | bytes accessed | tf_op | source)
XLA Modules:
  0.0 110.4 jit_solution(17771439975469802644)
XLA Ops:
  0.0 2.5 %collective-permute-start.3 = (bf16[64,4096]{1,0:T(8,128)(2,1)}, bf16[64,4096]{1,0:T(8,128)(2,1)}, u32[]{:S(2)}, u32[]{:S(2)}) collective-permute-start(bf16[64,4096]{1,0:T(8,128)(2,1)} %refs_0_), channel_id=1, source_target_pairs={{0,1},{1,2},{2,3},{3,4},{4,5},{5,6},{6,7},{7,0},{8,9},{9,10},{10,1... | collective-permute-start | bytes 1572872 | tf_op jit(solution)/shard_map/ppermute | solution.py:37
  2.6 4.0 %collective-permute-start.5 = (bf16[64,4096]{1,0:T(8,128)(2,1)}, bf16[64,4096]{1,0:T(8,128)(2,1)}, u32[]{:S(2)}, u32[]{:S(2)}) collective-permute-start(bf16[64,4096]{1,0:T(8,128)(2,1)} %refs_0_), channel_id=1, source_target_pairs={{0,7},{1,0},{2,1},{3,2},{4,3},{5,4},{6,5},{7,6},{8,15},{9,8},{10,9... | collective-permute-start | bytes 1572872 | tf_op jit(solution)/shard_map/ppermute | solution.py:37
  8.0 1.2 %copy.20 = bf16[2,1024,128]{1,2,0:T(8,128)(2,1)S(1)} copy(bf16[2,1024,128]{2,1,0:T(8,128)(2,1)} %bitcast.68) | data formatting | bytes 1048576 | tf_op jit(solution)/shard_map/reshape | solution.py:514
  9.3 3.0 %collective-permute-start.2 = (bf16[272,1024]{1,0:T(8,128)(2,1)S(1)}, bf16[272,1024]{1,0:T(8,128)(2,1)S(1)}, u32[]{:S(2)}, u32[]{:S(2)}) collective-permute-start(bf16[272,1024]{1,0:T(8,128)(2,1)S(1)} %fusion.1.refs_0_), channel_id=1, source_target_pairs={{0,32},{8,136},{16,48},{24,152},{32,0},{40,168},{48,16},{56,184},{... | collective-permute-start | bytes 1671176 | tf_op jit(solution)/shard_map/ppermute | solution.py:41
  17.4 1.6 %copy.28 = bf16[512,8,2,128]{3,1,2,0:T(8,128)(2,1)} copy(bf16[512,8,2,128]{3,2,1,0:T(2,128)(2,1)S(1)} %bitcast.64) | data formatting | bytes 4194304
  19.8 2.7 %collective-permute-start.6 = (bf16[64,4096]{1,0:T(8,128)(2,1)}, bf16[64,4096]{1,0:T(8,128)(2,1)S(1)}, u32[]{:S(2)}, u32[]{:S(2)}) collective-permute-start(bf16[64,4096]{1,0:T(8,128)(2,1)} %collective-permute-done.5.refs_2_), channel_id=1, source_target_pairs={{0,7},{1,0},{2,1},{3,2},{4,3},{5,4},{6,5},{7,6},{8,15},{9,8},{10,9... | collective-permute-start | bytes 1572872 | tf_op jit(solution)/shard_map/ppermute | solution.py:37
  24.3 1.8 %collective-permute-done.1.refs_2_ = bf16[272,1024]{1,0:T(8,128)(2,1)} collective-permute-done((bf16[272,1024]{1,0:T(8,128)(2,1)S(1)}, bf16[272,1024]{1,0:T(8,128)(2,1)}, u32[]{:S(2)}, u32[]{:S(2)}) %collective-permute-start.1) | collective-permute-done | bytes 557088 | tf_op jit(solution)/shard_map/ppermute | solution.py:41
  26.1 3.0 %lined.1 = (bf16[1088,1024]{1,0:T(8,128)(2,1)}, bf16[64,1024]{1,0:T(8,128)(2,1)}) custom-call(bf16[272,1024]{1,0:T(8,128)(2,1)} %copy-done.3, bf16[272,1024]{1,0:T(8,128)(2,1)} %collective-permute-done.refs_1_, bf16[272,1024]{1,0:T(8,128)(2,1)} %collective-permute-done.1.refs_2_, bf16[272,1024]{1,0:T(8,128)(2,1)} %copy-done.5), custom_call_target="tpu_custom_call" | custom-call | bytes 4000000 | tf_op jit(solution)/shard_map/lined/pallas_call | solution.py:62
  29.1 4.0 %collective-permute-done.4.refs_3_ = bf16[64,4096]{1,0:T(8,128)(2,1)} collective-permute-done((bf16[64,4096]{1,0:T(8,128)(2,1)}, bf16[64,4096]{1,0:T(8,128)(2,1)}, u32[]{:S(2)}, u32[]{:S(2)}) %collective-permute-start.4) | collective-permute-done | bytes 524320 | tf_op jit(solution)/shard_map/ppermute | solution.py:37
  33.1 4.6 %collective-permute-start.9 = (bf16[64,1024]{1,0:T(8,128)(2,1)}, bf16[64,1024]{1,0:T(8,128)(2,1)S(1)}, u32[]{:S(2)}, u32[]{:S(2)}) collective-permute-start(bf16[64,1024]{1,0:T(8,128)(2,1)} %get-tuple-element.67.refs_0_), channel_id=1, source_target_pairs={{0,128},{8,40},{16,144},{24,56},{32,160},{40,8},{48,176},{56,24},{... | collective-permute-start | bytes 393224 | tf_op jit(solution)/shard_map/ppermute | solution.py:41
  37.7 1.5 %collective-permute-start.7 = (bf16[1088,1024]{1,0:T(8,128)(2,1)}, bf16[1088,1024]{1,0:T(8,128)(2,1)}, u32[]{:S(2)}, u32[]{:S(2)}) collective-permute-start(bf16[1088,1024]{1,0:T(8,128)(2,1)} %get-tuple-element.90.s0), channel_id=1, source_target_pairs={{0,64},{8,24},{16,80},{24,40},{32,96},{40,56},{48,112},{56,8},{64,... | collective-permute-start | bytes 6684680 | tf_op jit(solution)/shard_map/ppermute | solution.py:41
  39.1 2.7 %collective-permute-start.11 = (bf16[64,4096]{1,0:T(8,128)(2,1)}, bf16[64,4096]{1,0:T(8,128)(2,1)S(1)}, u32[]{:S(2)}, u32[]{:S(2)}) collective-permute-start(bf16[64,4096]{1,0:T(8,128)(2,1)} %copy-done.15), channel_id=1, source_target_pairs={{0,7},{1,0},{2,1},{3,2},{4,3},{5,4},{6,5},{7,6},{8,15},{9,8},{10,9... | collective-permute-start | bytes 1572872 | tf_op jit(solution)/shard_map/ppermute | solution.py:37
  41.8 1.0 collective-permute-start.16
  42.8 7.9 %project.2 = (bf16[320,1024]{1,0:T(8,128)(2,1)}, bf16[320,384]{1,0:T(8,128)(2,1)}) custom-call(bf16[64,4096]{1,0:T(8,128)(2,1)} %refs_0_, bf16[64,4096]{1,0:T(8,128)(2,1)} %collective-permute-done.3.refs_1_, bf16[64,4096]{1,0:T(8,128)(2,1)} %collective-permute-done.5.refs_2_, bf16[64,4096]{1,0:T(8,128)(2,1)} %collective-permute-done.4.refs_3_, ...), custom_call_target="tpu_custom_call" | custom-call | flops 24000000000 | bytes 14000000 | tf_op jit(solution)/shard_map/project/pallas_call | solution.py:389
  50.7 3.0 %collective-permute-done.10.refs_0_ = bf16[64,4096]{1,0:T(8,128)(2,1)S(1)} collective-permute-done((bf16[64,4096]{1,0:T(8,128)(2,1)}, bf16[64,4096]{1,0:T(8,128)(2,1)S(1)}, u32[]{:S(2)}, u32[]{:S(2)}) %collective-permute-start.10) | collective-permute-done | bytes 524320 | tf_op jit(solution)/shard_map/ppermute | solution.py:37
  54.7 1.8 %halves.3 = (bf16[32,4096]{1,0:T(8,128)(2,1)}, bf16[32,4096]{1,0:T(8,128)(2,1)}) custom-call(bf16[64,4096]{1,0:T(8,128)(2,1)} %copy-done.6, bf16[64,4096]{1,0:T(8,128)(2,1)} %copy-done.7), custom_call_target="tpu_custom_call" | custom-call | bytes 4000000 | tf_op jit(solution)/shard_map/halves/pallas_call | solution.py:62
  56.5 1.3 %collective-permute-start.14 = (bf16[32,4096]{1,0:T(8,128)(2,1)}, bf16[32,4096]{1,0:T(8,128)(2,1)S(1)}, u32[]{:S(2)}, u32[]{:S(2)}) collective-permute-start(bf16[32,4096]{1,0:T(8,128)(2,1)} %get-tuple-element.88), channel_id=1, source_target_pairs={{0,1},{1,2},{2,3},{3,4},{4,5},{5,6},{6,7},{7,0},{8,9},{9,10},{10,1... | collective-permute-start | bytes 786440 | tf_op jit(solution)/shard_map/ppermute | solution.py:37
  57.8 1.5 %collective-permute-start.15 = (bf16[32,4096]{1,0:T(8,128)(2,1)}, bf16[32,4096]{1,0:T(8,128)(2,1)S(1)}, u32[]{:S(2)}, u32[]{:S(2)}) collective-permute-start(bf16[32,4096]{1,0:T(8,128)(2,1)} %get-tuple-element.89), channel_id=1, source_target_pairs={{0,7},{1,0},{2,1},{3,2},{4,3},{5,4},{6,5},{7,6},{8,15},{9,8},{10,9... | collective-permute-start | bytes 786440 | tf_op jit(solution)/shard_map/ppermute | solution.py:37
  59.3 5.3 %collective-permute-done.8.refs_1_.refs_2_.s3 = bf16[1088,1024]{1,0:T(8,128)(2,1)S(1)} collective-permute-done((bf16[1088,1024]{1,0:T(8,128)(2,1)}, bf16[1088,1024]{1,0:T(8,128)(2,1)S(1)}, u32[]{:S(2)}, u32[]{:S(2)}) %collective-permute-start.8) | collective-permute-done | bytes 2228256 | tf_op jit(solution)/shard_map/ppermute | solution.py:41
  64.6 1.2 %collective-permute-done.7.refs_0_.refs_1_.s2 = bf16[1088,1024]{1,0:T(8,128)(2,1)} collective-permute-done((bf16[1088,1024]{1,0:T(8,128)(2,1)}, bf16[1088,1024]{1,0:T(8,128)(2,1)}, u32[]{:S(2)}, u32[]{:S(2)}) %collective-permute-start.7) | collective-permute-done | bytes 2228256 | tf_op jit(solution)/shard_map/ppermute | solution.py:41
  65.9 2.6 %halves.2 = (bf16[512,1024]{1,0:T(8,128)(2,1)}, bf16[512,1024]{1,0:T(8,128)(2,1)}) custom-call(bf16[1088,1024]{1,0:T(8,128)(2,1)} %collective-permute-done.7.refs_0_.refs_1_.s2, bf16[1088,1024]{1,0:T(8,128)(2,1)} %copy-done.2), custom_call_target="tpu_custom_call" | custom-call | bytes 4000000 | tf_op jit(solution)/shard_map/halves/pallas_call | solution.py:62
  68.5 1.8 %gathered_priors.1.p0 = bf16[256,1024]{1,0:T(8,128)(2,1)} custom-call(bf16[64,1024]{1,0:T(8,128)(2,1)} %get-tuple-element.67.refs_0_, bf16[1088,1024]{1,0:T(8,128)(2,1)} %collective-permute-done.7.refs_0_.refs_1_.s2, bf16[1088,1024]{1,0:T(8,128)(2,1)} %copy-done.2, bf16[64,1024]{1,0:T(8,128)(2,1)} %copy-done.8), custom_call_target="tpu_custom_call" | custom-call | bytes 4000000 | tf_op jit(solution)/shard_map/gathered_priors/pallas_call | solution.py:62
  70.3 2.1 %collective-permute-start.17 = (bf16[256,1024]{1,0:T(8,128)(2,1)}, bf16[256,1024]{1,0:T(8,128)(2,1)S(1)}, u32[]{:S(2)}, u32[]{:S(2)}) collective-permute-start(bf16[256,1024]{1,0:T(8,128)(2,1)} %gathered_priors.1.p0), channel_id=1, source_target_pairs={{0,8},{8,0},{16,24},{24,16},{32,40},{40,32},{48,56},{56,48},{64,72... | collective-permute-start | bytes 1572872 | tf_op jit(solution)/shard_map/ppermute | solution.py:41
  72.4 1.2 %collective-permute-start.12 = (bf16[512,1024]{1,0:T(8,128)(2,1)}, bf16[512,1024]{1,0:T(8,128)(2,1)S(1)}, u32[]{:S(2)}, u32[]{:S(2)}) collective-permute-start(bf16[512,1024]{1,0:T(8,128)(2,1)} %get-tuple-element.85), channel_id=1, source_target_pairs={{0,64},{8,24},{16,80},{24,40},{32,96},{40,56},{48,112},{56,8},{64,... | collective-permute-start | bytes 3145736 | tf_op jit(solution)/shard_map/ppermute | solution.py:41
  73.6 1.5 %collective-permute-start.13 = (bf16[512,1024]{1,0:T(8,128)(2,1)}, bf16[512,1024]{1,0:T(8,128)(2,1)}, u32[]{:S(2)}, u32[]{:S(2)}) collective-permute-start(bf16[512,1024]{1,0:T(8,128)(2,1)} %get-tuple-element.86), channel_id=1, source_target_pairs={{0,192},{8,56},{16,208},{24,8},{32,224},{40,24},{48,240},{56,40},{... | collective-permute-start | bytes 3145736 | tf_op jit(solution)/shard_map/ppermute | solution.py:41
  75.8 6.4 %project.3 = (bf16[192,1024]{1,0:T(8,128)(2,1)}, bf16[192,384]{1,0:T(8,128)(2,1)}) custom-call(bf16[64,4096]{1,0:T(8,128)(2,1)} %copy-done.6, bf16[64,4096]{1,0:T(8,128)(2,1)} %copy-done.7, bf16[32,4096]{1,0:T(8,128)(2,1)} %copy-done.17, bf16[32,4096]{1,0:T(8,128)(2,1)} %copy-done.18, bf16[4096,1024]{1,0:T(8,128)(2,1)} %refs_4_, bf16[4096,256]{1,0:T(8,128)(2,1)} %bitcast.66, ...), custom_call_target="tpu_custom_call" | custom-call | flops 24000000000 | bytes 14000000 | tf_op jit(solution)/shard_map/project/pallas_call | solution.py:389
  83.1 0.8 copy-done.16
  83.9 14.9 %mixer_inner.1.refs_7_ = f32[10,544,128]{2,1,0:T(8,128)} custom-call(s32[1]{0:T(128)} %bitcast.12.where, s32[4,33]{1,0:T(4,128)} %pad.25.table.refs_0_, bf16[1088,1024]{1,0:T(8,128)(2,1)} %get-tuple-element.90.s0, bf16[1088,1024]{1,0:T(8,128)(2,1)} %collective-permute-done.16.s1, bf16[1088,1024]{1,0:T(8,128)(2,1)} %collective-permute-done.7.refs_0_.refs_1_.s2, ...), custom_call_target="tpu_custom_call" | custom-call | flops 14000000000 | bytes 18000000 | tf_op jit(solution)/shard_map/mixer_inner/pallas_call | solution.py:408
  99.4 2.5 %collective-permute-done.20.refs_4_ = bf16[512,1024]{1,0:T(8,128)(2,1)S(1)} collective-permute-done((bf16[512,1024]{1,0:T(8,128)(2,1)S(1)}, bf16[512,1024]{1,0:T(8,128)(2,1)S(1)}, u32[]{:S(2)}, u32[]{:S(2)}) %collective-permute-start.20) | collective-permute-done | bytes 1048608 | tf_op jit(solution)/shard_map/ppermute | solution.py:41
  102.0 1.4 %collective-permute-done.21.refs_6_ = bf16[512,1024]{1,0:T(8,128)(2,1)S(1)} collective-permute-done((bf16[512,1024]{1,0:T(8,128)(2,1)}, bf16[512,1024]{1,0:T(8,128)(2,1)S(1)}, u32[]{:S(2)}, u32[]{:S(2)}) %collective-permute-start.21) | collective-permute-done | bytes 1048608 | tf_op jit(solution)/shard_map/ppermute | solution.py:41
  103.3 1.8 %copy-done = f32[10,544,128]{2,1,0:T(8,128)S(1)} copy-done((f32[10,544,128]{2,1,0:T(8,128)S(1)}, f32[10,544,128]{2,1,0:T(8,128)}, u32[]{:S(2)}) %copy-start) | copy-done | bytes 2785304
  105.1 5.1 %mixer_late.1 = bf16[512,1024]{1,0:T(8,128)(2,1)} custom-call(s32[4,33]{1,0:T(4,128)S(1)} %copy-done.1, bf16[1088,1024]{1,0:T(8,128)(2,1)S(1)} %collective-permute-done.18.refs_1_, bf16[1088,1024]{1,0:T(8,128)(2,1)} %collective-permute-done.19.refs_2_, bf16[512,1024]{1,0:T(8,128)(2,1)S(1)} %collective-permute-done.12.refs_3_, ...), custom_call_target="tpu_custom_call" | custom-call | flops 500000000 | bytes 13000000 | tf_op jit(solution)/shard_map/mixer_late/pallas_call | solution.py:434
  (87 shorter events, 12.3 us)
Async XLA Ops:
  0.0 13.8 %copy-start.12 = (s32[1,32]{1,0:T(1,128)S(1)}, s32[1,32]{1,0:T(1,128)}, u32[]{:S(2)}) copy-start(s32[1,32]{1,0:T(1,128)} %param.29) | copy-start | bytes 388
  0.0 13.9 %copy-start.10 = (bf16[4,2,128]{2,1,0:T(2,128)(2,1)S(1)}, bf16[4,2,128]{2,1,0:T(2,128)(2,1)}, u32[]{:S(2)}) copy-start(bf16[4,2,128]{2,1,0:T(2,128)(2,1)} %param.20) | copy-start | bytes 6148
  0.0 13.9 %copy-start.11 = (f32[16]{0:T(128)S(1)}, f32[16]{0:T(128)}, u32[]{:S(2)}) copy-start(f32[16]{0:T(128)} %param.23) | copy-start | bytes 196
  0.0 17.4 %copy-start.4 = (bf16[4096,2,128]{2,1,0:T(2,128)(2,1)S(1)}, bf16[4096,2,128]{2,1,0:T(2,128)(2,1)}, u32[]{:S(2)}) copy-start(bf16[4096,2,128]{2,1,0:T(2,128)(2,1)} %param.17) | copy-start | bytes 6291460
  0.0 19.7 %collective-permute-start.3 = (bf16[64,4096]{1,0:T(8,128)(2,1)}, bf16[64,4096]{1,0:T(8,128)(2,1)}, u32[]{:S(2)}, u32[]{:S(2)}) collective-permute-start(bf16[64,4096]{1,0:T(8,128)(2,1)} %refs_0_), channel_id=1, source_target_pairs={{0,1},{1,2},{2,3},{3,4},{4,5},{5,6},{6,7},{7,0},{8,9},{9,10},{10,1... | collective-permute-start | bytes 1572872 | tf_op jit(solution)/shard_map/ppermute | solution.py:37
  2.6 17.2 %collective-permute-start.5 = (bf16[64,4096]{1,0:T(8,128)(2,1)}, bf16[64,4096]{1,0:T(8,128)(2,1)}, u32[]{:S(2)}, u32[]{:S(2)}) collective-permute-start(bf16[64,4096]{1,0:T(8,128)(2,1)} %refs_0_), channel_id=1, source_target_pairs={{0,7},{1,0},{2,1},{3,2},{4,3},{5,4},{6,5},{7,6},{8,15},{9,8},{10,9... | collective-permute-start | bytes 1572872 | tf_op jit(solution)/shard_map/ppermute | solution.py:37
  9.3 9.8 %copy-start.3 = (bf16[272,1024]{1,0:T(8,128)(2,1)}, bf16[272,1024]{1,0:T(8,128)(2,1)S(1)}, u32[]{:S(2)}) copy-start(bf16[272,1024]{1,0:T(8,128)(2,1)S(1)} %fusion.1.refs_0_) | copy-start | bytes 1671172
  9.3 14.9 %collective-permute-start.2 = (bf16[272,1024]{1,0:T(8,128)(2,1)S(1)}, bf16[272,1024]{1,0:T(8,128)(2,1)S(1)}, u32[]{:S(2)}, u32[]{:S(2)}) collective-permute-start(bf16[272,1024]{1,0:T(8,128)(2,1)S(1)} %fusion.1.refs_0_), channel_id=1, source_target_pairs={{0,32},{8,136},{16,48},{24,152},{32,0},{40,168},{48,16},{56,184},{... | collective-permute-start | bytes 1671176 | tf_op jit(solution)/shard_map/ppermute | solution.py:41
  12.3 13.7 %collective-permute-start.1 = (bf16[272,1024]{1,0:T(8,128)(2,1)S(1)}, bf16[272,1024]{1,0:T(8,128)(2,1)}, u32[]{:S(2)}, u32[]{:S(2)}) collective-permute-start(bf16[272,1024]{1,0:T(8,128)(2,1)S(1)} %fusion.1.refs_0_), channel_id=1, source_target_pairs={{0,48},{8,200},{16,0},{24,216},{32,16},{40,232},{48,32},{56,248},{... | collective-permute-start | bytes 1671176 | tf_op jit(solution)/shard_map/ppermute | solution.py:41
  13.1 13.0 %collective-permute-start = (bf16[272,1024]{1,0:T(8,128)(2,1)S(1)}, bf16[272,1024]{1,0:T(8,128)(2,1)}, u32[]{:S(2)}, u32[]{:S(2)}) collective-permute-start(bf16[272,1024]{1,0:T(8,128)(2,1)S(1)} %fusion.1.refs_0_), channel_id=1, source_target_pairs={{0,16},{8,72},{16,32},{24,88},{32,48},{40,104},{48,0},{56,120},{64... | collective-permute-start | bytes 1671176 | tf_op jit(solution)/shard_map/ppermute | solution.py:41
  17.4 5.6 %copy-start.14 = (f32[16]{0:T(128)S(1)}, f32[16]{0:T(128)}, u32[]{:S(2)}) copy-start(f32[16]{0:T(128)} %param.21) | copy-start | bytes 196
  17.4 6.2 %copy-start.9 = (bf16[4,1024]{1,0:T(4,128)(2,1)S(1)}, bf16[4,1024]{1,0:T(4,128)(2,1)}, u32[]{:S(2)}) copy-start(bf16[4,1024]{1,0:T(4,128)(2,1)} %param.19) | copy-start | bytes 24580
  19.7 13.4 %collective-permute-start.4 = (bf16[64,4096]{1,0:T(8,128)(2,1)}, bf16[64,4096]{1,0:T(8,128)(2,1)}, u32[]{:S(2)}, u32[]{:S(2)}) collective-permute-start(bf16[64,4096]{1,0:T(8,128)(2,1)} %collective-permute-done.3.refs_1_), channel_id=1, source_target_pairs={{0,1},{1,2},{2,3},{3,4},{4,5},{5,6},{6,7},{7,0},{8,9},{9,10},{10,1... | collective-permute-start | bytes 1572872 | tf_op jit(solution)/shard_map/ppermute | solution.py:37
  19.8 13.3 %collective-permute-start.6 = (bf16[64,4096]{1,0:T(8,128)(2,1)}, bf16[64,4096]{1,0:T(8,128)(2,1)S(1)}, u32[]{:S(2)}, u32[]{:S(2)}) collective-permute-start(bf16[64,4096]{1,0:T(8,128)(2,1)} %collective-permute-done.5.refs_2_), channel_id=1, source_target_pairs={{0,7},{1,0},{2,1},{3,2},{4,3},{5,4},{6,5},{7,6},{8,15},{9,8},{10,9... | collective-permute-start | bytes 1572872 | tf_op jit(solution)/shard_map/ppermute | solution.py:37
  33.1 6.0 %copy-start.15 = (bf16[64,4096]{1,0:T(8,128)(2,1)}, bf16[64,4096]{1,0:T(8,128)(2,1)S(1)}, u32[]{:S(2)}) copy-start(bf16[64,4096]{1,0:T(8,128)(2,1)S(1)} %collective-permute-done.6.refs_4_) | copy-start | bytes 1572868
  33.1 8.7 %collective-permute-start.9 = (bf16[64,1024]{1,0:T(8,128)(2,1)}, bf16[64,1024]{1,0:T(8,128)(2,1)S(1)}, u32[]{:S(2)}, u32[]{:S(2)}) collective-permute-start(bf16[64,1024]{1,0:T(8,128)(2,1)} %get-tuple-element.67.refs_0_), channel_id=1, source_target_pairs={{0,128},{8,40},{16,144},{24,56},{32,160},{40,8},{48,176},{56,24},{... | collective-permute-start | bytes 393224 | tf_op jit(solution)/shard_map/ppermute | solution.py:41
  37.6 26.9 %collective-permute-start.8 = (bf16[1088,1024]{1,0:T(8,128)(2,1)}, bf16[1088,1024]{1,0:T(8,128)(2,1)S(1)}, u32[]{:S(2)}, u32[]{:S(2)}) collective-permute-start(bf16[1088,1024]{1,0:T(8,128)(2,1)} %get-tuple-element.90.s0), channel_id=1, source_target_pairs={{0,192},{8,56},{16,208},{24,8},{32,224},{40,24},{48,240},{56,40},{... | collective-permute-start | bytes 6684680 | tf_op jit(solution)/shard_map/ppermute | solution.py:41
  37.7 28.1 %collective-permute-start.7 = (bf16[1088,1024]{1,0:T(8,128)(2,1)}, bf16[1088,1024]{1,0:T(8,128)(2,1)}, u32[]{:S(2)}, u32[]{:S(2)}) collective-permute-start(bf16[1088,1024]{1,0:T(8,128)(2,1)} %get-tuple-element.90.s0), channel_id=1, source_target_pairs={{0,64},{8,24},{16,80},{24,40},{32,96},{40,56},{48,112},{56,8},{64,... | collective-permute-start | bytes 6684680 | tf_op jit(solution)/shard_map/ppermute | solution.py:41
  39.1 14.6 %collective-permute-start.10 = (bf16[64,4096]{1,0:T(8,128)(2,1)}, bf16[64,4096]{1,0:T(8,128)(2,1)S(1)}, u32[]{:S(2)}, u32[]{:S(2)}) collective-permute-start(bf16[64,4096]{1,0:T(8,128)(2,1)} %collective-permute-done.4.refs_3_), channel_id=1, source_target_pairs={{0,1},{1,2},{2,3},{3,4},{4,5},{5,6},{6,7},{7,0},{8,9},{9,10},{10,1... | collective-permute-start | bytes 1572872 | tf_op jit(solution)/shard_map/ppermute | solution.py:37
  39.1 14.6 %collective-permute-start.11 = (bf16[64,4096]{1,0:T(8,128)(2,1)}, bf16[64,4096]{1,0:T(8,128)(2,1)S(1)}, u32[]{:S(2)}, u32[]{:S(2)}) collective-permute-start(bf16[64,4096]{1,0:T(8,128)(2,1)} %copy-done.15), channel_id=1, source_target_pairs={{0,7},{1,0},{2,1},{3,2},{4,3},{5,4},{6,5},{7,6},{8,15},{9,8},{10,9... | collective-permute-start | bytes 1572872 | tf_op jit(solution)/shard_map/ppermute | solution.py:37
  41.8 8.9 %copy-start.8 = (bf16[64,1024]{1,0:T(8,128)(2,1)}, bf16[64,1024]{1,0:T(8,128)(2,1)S(1)}, u32[]{:S(2)}) copy-start(bf16[64,1024]{1,0:T(8,128)(2,1)S(1)} %collective-permute-done.9.refs_3_) | copy-start | bytes 393220
  41.8 33.3 %collective-permute-start.16 = (bf16[1088,1024]{1,0:T(8,128)(2,1)}, bf16[1088,1024]{1,0:T(8,128)(2,1)}, u32[]{:S(2)}, u32[]{:S(2)}) collective-permute-start(bf16[1088,1024]{1,0:T(8,128)(2,1)} %get-tuple-element.90.s0), channel_id=1, source_target_pairs={{0,8},{8,0},{16,24},{24,16},{32,40},{40,32},{48,56},{56,48},{64,72... | collective-permute-start | bytes 6684680 | tf_op jit(solution)/shard_map/ppermute | solution.py:41
  56.5 17.1 %collective-permute-start.14 = (bf16[32,4096]{1,0:T(8,128)(2,1)}, bf16[32,4096]{1,0:T(8,128)(2,1)S(1)}, u32[]{:S(2)}, u32[]{:S(2)}) collective-permute-start(bf16[32,4096]{1,0:T(8,128)(2,1)} %get-tuple-element.88), channel_id=1, source_target_pairs={{0,1},{1,2},{2,3},{3,4},{4,5},{5,6},{6,7},{7,0},{8,9},{9,10},{10,1... | collective-permute-start | bytes 786440 | tf_op jit(solution)/shard_map/ppermute | solution.py:37
  57.8 17.4 %collective-permute-start.15 = (bf16[32,4096]{1,0:T(8,128)(2,1)}, bf16[32,4096]{1,0:T(8,128)(2,1)S(1)}, u32[]{:S(2)}, u32[]{:S(2)}) collective-permute-start(bf16[32,4096]{1,0:T(8,128)(2,1)} %get-tuple-element.89), channel_id=1, source_target_pairs={{0,7},{1,0},{2,1},{3,2},{4,3},{5,4},{6,5},{7,6},{8,15},{9,8},{10,9... | collective-permute-start | bytes 786440 | tf_op jit(solution)/shard_map/ppermute | solution.py:37
  70.3 12.8 %collective-permute-start.17 = (bf16[256,1024]{1,0:T(8,128)(2,1)}, bf16[256,1024]{1,0:T(8,128)(2,1)S(1)}, u32[]{:S(2)}, u32[]{:S(2)}) collective-permute-start(bf16[256,1024]{1,0:T(8,128)(2,1)} %gathered_priors.1.p0), channel_id=1, source_target_pairs={{0,8},{8,0},{16,24},{24,16},{32,40},{40,32},{48,56},{56,48},{64,72... | collective-permute-start | bytes 1572872 | tf_op jit(solution)/shard_map/ppermute | solution.py:41
  72.4 26.4 %collective-permute-start.12 = (bf16[512,1024]{1,0:T(8,128)(2,1)}, bf16[512,1024]{1,0:T(8,128)(2,1)S(1)}, u32[]{:S(2)}, u32[]{:S(2)}) collective-permute-start(bf16[512,1024]{1,0:T(8,128)(2,1)} %get-tuple-element.85), channel_id=1, source_target_pairs={{0,64},{8,24},{16,80},{24,40},{32,96},{40,56},{48,112},{56,8},{64,... | collective-permute-start | bytes 3145736 | tf_op jit(solution)/shard_map/ppermute | solution.py:41
  73.6 25.2 %collective-permute-start.13 = (bf16[512,1024]{1,0:T(8,128)(2,1)}, bf16[512,1024]{1,0:T(8,128)(2,1)}, u32[]{:S(2)}, u32[]{:S(2)}) collective-permute-start(bf16[512,1024]{1,0:T(8,128)(2,1)} %get-tuple-element.86), channel_id=1, source_target_pairs={{0,192},{8,56},{16,208},{24,8},{32,224},{40,24},{48,240},{56,40},{... | collective-permute-start | bytes 3145736 | tf_op jit(solution)/shard_map/ppermute | solution.py:41
  82.2 21.1 %collective-permute-start.18 = (bf16[1088,1024]{1,0:T(8,128)(2,1)}, bf16[1088,1024]{1,0:T(8,128)(2,1)S(1)}, u32[]{:S(2)}, u32[]{:S(2)}) collective-permute-start(bf16[1088,1024]{1,0:T(8,128)(2,1)} %collective-permute-done.7.refs_0_.refs_1_.s2), channel_id=1, source_target_pairs={{0,8},{8,0},{16,24},{24,16},{32,40},{40,32},{48,56},{56,48},{64,72... | collective-permute-start | bytes 6684680 | tf_op jit(solution)/shard_map/ppermute | solution.py:41
  83.0 20.4 %collective-permute-start.19 = (bf16[1088,1024]{1,0:T(8,128)(2,1)}, bf16[1088,1024]{1,0:T(8,128)(2,1)}, u32[]{:S(2)}, u32[]{:S(2)}) collective-permute-start(bf16[1088,1024]{1,0:T(8,128)(2,1)} %copy-done.2), channel_id=1, source_target_pairs={{0,8},{8,0},{16,24},{24,16},{32,40},{40,32},{48,56},{56,48},{64,72... | collective-permute-start | bytes 6684680 | tf_op jit(solution)/shard_map/ppermute | solution.py:41
  83.9 19.4 %copy-start.1 = (s32[4,33]{1,0:T(4,128)S(1)}, s32[4,33]{1,0:T(4,128)}, u32[]{:S(2)}) copy-start(s32[4,33]{1,0:T(4,128)} %pad.25.table.refs_0_) | copy-start | bytes 1588
  98.8 3.1 %collective-permute-start.20 = (bf16[512,1024]{1,0:T(8,128)(2,1)S(1)}, bf16[512,1024]{1,0:T(8,128)(2,1)S(1)}, u32[]{:S(2)}, u32[]{:S(2)}) collective-permute-start(bf16[512,1024]{1,0:T(8,128)(2,1)S(1)} %collective-permute-done.12.refs_3_), channel_id=1, source_target_pairs={{0,8},{8,0},{16,24},{24,16},{32,40},{40,32},{48,56},{56,48},{64,72... | collective-permute-start | bytes 3145736 | tf_op jit(solution)/shard_map/ppermute | solution.py:41
  99.3 4.0 %collective-permute-start.21 = (bf16[512,1024]{1,0:T(8,128)(2,1)}, bf16[512,1024]{1,0:T(8,128)(2,1)S(1)}, u32[]{:S(2)}, u32[]{:S(2)}) collective-permute-start(bf16[512,1024]{1,0:T(8,128)(2,1)} %collective-permute-done.13.refs_5_), channel_id=1, source_target_pairs={{0,8},{8,0},{16,24},{24,16},{32,40},{40,32},{48,56},{56,48},{64,72... | collective-permute-start | bytes 3145736 | tf_op jit(solution)/shard_map/ppermute | solution.py:41
  (9 other events, 15.4 us)

commit v3 on v2

--- a/solution.py
+++ b/solution.py
@@ -295,7 +295,7 @@
             sum_ref[pair, pl.ds(at, TILE), :] = out + skip[:, here] * x_w[TILE:].astype(F32)
         return carry
 
-    lax.fori_loop(0, rows // TILE, tile, 0)
+    lax.fori_loop(0, rows // TILE, tile, 0, unroll=2)
     sum_ref[0 : x_cols // 128, rows:, :] = jnp.zeros((x_cols // 128, sum_ref.shape[1] - rows, 128), F32)
     fade_ref[rows:, :] = jnp.zeros((fade_ref.shape[0] - rows, 128), F32)
     add_carried(table, 0, parts, c_ref, fade_ref, states, sum_ref, state_sem)
@@ -319,7 +319,7 @@
     row = lax.broadcasted_iota(jnp.int32, (32, 128), 0)
     lane_head = lax.broadcasted_iota(jnp.int32, (128, x_cols), 1) // 64
     spread = jnp.where(lane_head == lax.broadcasted_iota(jnp.int32, (128, x_cols), 0), 1.0, 0.0).astype(BF16)
-    side = 4
+    side = 8
 
     def some(group, carry):
         picks = []

time: 111 us -> 111 us (level)
    pallas_call x1, Pallas kernels: 14.9 us -> 13.8 us  [mixer_inner(): pl.pallas_call(inner_kernel, out_shape=jax.ShapeDtypeStruct((x_cols // 12...]
  transfers between devices with their start and end apart: 22 -> 22, of which waited for: 7 -> 7; matrix products, arithmetic and copies ran while one was open for 9% -> 9% of each run, Pallas kernels for 35% -> 34%
where the time goes in v3:
time: 111 us
  Pallas kernels  43.1 us (39%)
  starting transfers between devices  33.6 us (30%)
  waiting for transfers between devices  19.2 us (17%)
  local copies, waits for them, and re-layouts  12 us (11%)
  other arithmetic  2.78 us (3%)
    ppermute x14, starting transfers between devices, on_cache(): return lax.ppermute(value, 'cache', pairs)  18.8 us
    ppermute x8, starting transfers between devices, over_z(): return lax.ppermute(value, 'tp', [(z, (z + step) % NZ) for z in range(NZ)])  14.7 us
    pallas_call x2, Pallas kernels, project(): pl.pallas_call(project_kernel, out_shape=(jax.ShapeDtypeStruct((rows, x_c...  14.2 us
    pallas_call x1, Pallas kernels, mixer_inner(): pl.pallas_call(inner_kernel, out_shape=jax.ShapeDtypeStruct((x_cols // 12...  13.8 us
    ppermute x14, waiting for transfers between devices, on_cache(): return lax.ppermute(value, 'cache', pairs)  12.2 us
    pallas_call x4, Pallas kernels, moved(): pl.pallas_call(kernel, out_shape=[jax.ShapeDtypeStruct(shape, sources[0]....  9.22 us
    unnamed x42, local copies, waits for them, and re-layouts  7.51 us
    ppermute x8, waiting for transfers between devices, over_z(): return lax.ppermute(value, 'tp', [(z, (z + step) % NZ) for z in range(NZ)])  6.99 us
  transfers between devices with their start and end apart: 22, of which 7 were waited for; matrix products, arithmetic and copies ran while one was open for 9% of the time, Pallas kernels for 34%

profile of v3, /device:TPU:1, one launch (start us, length us, event | category | flops | bytes accessed | tf_op | source)
XLA Modules:
  0.0 111.1 jit_solution(11918145354007842744)
XLA Ops:
  0.0 2.5 %collective-permute-start.3 = (bf16[64,4096]{1,0:T(8,128)(2,1)}, bf16[64,4096]{1,0:T(8,128)(2,1)}, u32[]{:S(2)}, u32[]{:S(2)}) collective-permute-start(bf16[64,4096]{1,0:T(8,128)(2,1)} %refs_0_), channel_id=1, source_target_pairs={{0,1},{1,2},{2,3},{3,4},{4,5},{5,6},{6,7},{7,0},{8,9},{9,10},{10,1... | collective-permute-start | bytes 1572872 | tf_op jit(solution)/shard_map/ppermute | solution.py:37
  2.6 4.0 %collective-permute-start.5 = (bf16[64,4096]{1,0:T(8,128)(2,1)}, bf16[64,4096]{1,0:T(8,128)(2,1)}, u32[]{:S(2)}, u32[]{:S(2)}) collective-permute-start(bf16[64,4096]{1,0:T(8,128)(2,1)} %refs_0_), channel_id=1, source_target_pairs={{0,7},{1,0},{2,1},{3,2},{4,3},{5,4},{6,5},{7,6},{8,15},{9,8},{10,9... | collective-permute-start | bytes 1572872 | tf_op jit(solution)/shard_map/ppermute | solution.py:37
  8.0 1.2 %copy.20 = bf16[2,1024,128]{1,2,0:T(8,128)(2,1)S(1)} copy(bf16[2,1024,128]{2,1,0:T(8,128)(2,1)} %bitcast.68) | data formatting | bytes 1048576 | tf_op jit(solution)/shard_map/reshape | solution.py:514
  9.3 3.0 %collective-permute-start.2 = (bf16[272,1024]{1,0:T(8,128)(2,1)S(1)}, bf16[272,1024]{1,0:T(8,128)(2,1)S(1)}, u32[]{:S(2)}, u32[]{:S(2)}) collective-permute-start(bf16[272,1024]{1,0:T(8,128)(2,1)S(1)} %fusion.1.refs_0_), channel_id=1, source_target_pairs={{0,32},{8,136},{16,48},{24,152},{32,0},{40,168},{48,16},{56,184},{... | collective-permute-start | bytes 1671176 | tf_op jit(solution)/shard_map/ppermute | solution.py:41
  17.4 1.6 %copy.28 = bf16[512,8,2,128]{3,1,2,0:T(8,128)(2,1)} copy(bf16[512,8,2,128]{3,2,1,0:T(2,128)(2,1)S(1)} %bitcast.64) | data formatting | bytes 4194304
  19.8 2.7 %collective-permute-start.6 = (bf16[64,4096]{1,0:T(8,128)(2,1)}, bf16[64,4096]{1,0:T(8,128)(2,1)S(1)}, u32[]{:S(2)}, u32[]{:S(2)}) collective-permute-start(bf16[64,4096]{1,0:T(8,128)(2,1)} %collective-permute-done.5.refs_2_), channel_id=1, source_target_pairs={{0,7},{1,0},{2,1},{3,2},{4,3},{5,4},{6,5},{7,6},{8,15},{9,8},{10,9... | collective-permute-start | bytes 1572872 | tf_op jit(solution)/shard_map/ppermute | solution.py:37
  24.3 1.8 %collective-permute-done.1.refs_2_ = bf16[272,1024]{1,0:T(8,128)(2,1)} collective-permute-done((bf16[272,1024]{1,0:T(8,128)(2,1)S(1)}, bf16[272,1024]{1,0:T(8,128)(2,1)}, u32[]{:S(2)}, u32[]{:S(2)}) %collective-permute-start.1) | collective-permute-done | bytes 557088 | tf_op jit(solution)/shard_map/ppermute | solution.py:41
  26.1 3.0 %lined.1 = (bf16[1088,1024]{1,0:T(8,128)(2,1)}, bf16[64,1024]{1,0:T(8,128)(2,1)}) custom-call(bf16[272,1024]{1,0:T(8,128)(2,1)} %copy-done.3, bf16[272,1024]{1,0:T(8,128)(2,1)} %collective-permute-done.refs_1_, bf16[272,1024]{1,0:T(8,128)(2,1)} %collective-permute-done.1.refs_2_, bf16[272,1024]{1,0:T(8,128)(2,1)} %copy-done.5), custom_call_target="tpu_custom_call" | custom-call | bytes 4000000 | tf_op jit(solution)/shard_map/lined/pallas_call | solution.py:62
  29.1 4.0 %collective-permute-done.4.refs_3_ = bf16[64,4096]{1,0:T(8,128)(2,1)} collective-permute-done((bf16[64,4096]{1,0:T(8,128)(2,1)}, bf16[64,4096]{1,0:T(8,128)(2,1)}, u32[]{:S(2)}, u32[]{:S(2)}) %collective-permute-start.4) | collective-permute-done | bytes 524320 | tf_op jit(solution)/shard_map/ppermute | solution.py:37
  33.1 4.6 %collective-permute-start.9 = (bf16[64,1024]{1,0:T(8,128)(2,1)}, bf16[64,1024]{1,0:T(8,128)(2,1)S(1)}, u32[]{:S(2)}, u32[]{:S(2)}) collective-permute-start(bf16[64,1024]{1,0:T(8,128)(2,1)} %get-tuple-element.67.refs_0_), channel_id=1, source_target_pairs={{0,128},{8,40},{16,144},{24,56},{32,160},{40,8},{48,176},{56,24},{... | collective-permute-start | bytes 393224 | tf_op jit(solution)/shard_map/ppermute | solution.py:41
  37.7 1.5 %collective-permute-start.7 = (bf16[1088,1024]{1,0:T(8,128)(2,1)}, bf16[1088,1024]{1,0:T(8,128)(2,1)}, u32[]{:S(2)}, u32[]{:S(2)}) collective-permute-start(bf16[1088,1024]{1,0:T(8,128)(2,1)} %get-tuple-element.90.s0), channel_id=1, source_target_pairs={{0,64},{8,24},{16,80},{24,40},{32,96},{40,56},{48,112},{56,8},{64,... | collective-permute-start | bytes 6684680 | tf_op jit(solution)/shard_map/ppermute | solution.py:41
  39.1 2.7 %collective-permute-start.11 = (bf16[64,4096]{1,0:T(8,128)(2,1)}, bf16[64,4096]{1,0:T(8,128)(2,1)S(1)}, u32[]{:S(2)}, u32[]{:S(2)}) collective-permute-start(bf16[64,4096]{1,0:T(8,128)(2,1)} %copy-done.15), channel_id=1, source_target_pairs={{0,7},{1,0},{2,1},{3,2},{4,3},{5,4},{6,5},{7,6},{8,15},{9,8},{10,9... | collective-permute-start | bytes 1572872 | tf_op jit(solution)/shard_map/ppermute | solution.py:37
  41.8 1.0 collective-permute-start.16
  42.8 7.9 %project.2 = (bf16[320,1024]{1,0:T(8,128)(2,1)}, bf16[320,384]{1,0:T(8,128)(2,1)}) custom-call(bf16[64,4096]{1,0:T(8,128)(2,1)} %refs_0_, bf16[64,4096]{1,0:T(8,128)(2,1)} %collective-permute-done.3.refs_1_, bf16[64,4096]{1,0:T(8,128)(2,1)} %collective-permute-done.5.refs_2_, bf16[64,4096]{1,0:T(8,128)(2,1)} %collective-permute-done.4.refs_3_, ...), custom_call_target="tpu_custom_call" | custom-call | flops 24000000000 | bytes 14000000 | tf_op jit(solution)/shard_map/project/pallas_call | solution.py:389
  50.7 3.0 %collective-permute-done.10.refs_0_ = bf16[64,4096]{1,0:T(8,128)(2,1)S(1)} collective-permute-done((bf16[64,4096]{1,0:T(8,128)(2,1)}, bf16[64,4096]{1,0:T(8,128)(2,1)S(1)}, u32[]{:S(2)}, u32[]{:S(2)}) %collective-permute-start.10) | collective-permute-done | bytes 524320 | tf_op jit(solution)/shard_map/ppermute | solution.py:37
  54.7 1.8 %halves.3 = (bf16[32,4096]{1,0:T(8,128)(2,1)}, bf16[32,4096]{1,0:T(8,128)(2,1)}) custom-call(bf16[64,4096]{1,0:T(8,128)(2,1)} %copy-done.6, bf16[64,4096]{1,0:T(8,128)(2,1)} %copy-done.7), custom_call_target="tpu_custom_call" | custom-call | bytes 4000000 | tf_op jit(solution)/shard_map/halves/pallas_call | solution.py:62
  56.5 1.3 %collective-permute-start.14 = (bf16[32,4096]{1,0:T(8,128)(2,1)}, bf16[32,4096]{1,0:T(8,128)(2,1)S(1)}, u32[]{:S(2)}, u32[]{:S(2)}) collective-permute-start(bf16[32,4096]{1,0:T(8,128)(2,1)} %get-tuple-element.88), channel_id=1, source_target_pairs={{0,1},{1,2},{2,3},{3,4},{4,5},{5,6},{6,7},{7,0},{8,9},{9,10},{10,1... | collective-permute-start | bytes 786440 | tf_op jit(solution)/shard_map/ppermute | solution.py:37
  57.8 1.5 %collective-permute-start.15 = (bf16[32,4096]{1,0:T(8,128)(2,1)}, bf16[32,4096]{1,0:T(8,128)(2,1)S(1)}, u32[]{:S(2)}, u32[]{:S(2)}) collective-permute-start(bf16[32,4096]{1,0:T(8,128)(2,1)} %get-tuple-element.89), channel_id=1, source_target_pairs={{0,7},{1,0},{2,1},{3,2},{4,3},{5,4},{6,5},{7,6},{8,15},{9,8},{10,9... | collective-permute-start | bytes 786440 | tf_op jit(solution)/shard_map/ppermute | solution.py:37
  59.3 5.3 %collective-permute-done.8.refs_1_.refs_2_.s3 = bf16[1088,1024]{1,0:T(8,128)(2,1)S(1)} collective-permute-done((bf16[1088,1024]{1,0:T(8,128)(2,1)}, bf16[1088,1024]{1,0:T(8,128)(2,1)S(1)}, u32[]{:S(2)}, u32[]{:S(2)}) %collective-permute-start.8) | collective-permute-done | bytes 2228256 | tf_op jit(solution)/shard_map/ppermute | solution.py:41
  64.6 1.2 %collective-permute-done.7.refs_0_.refs_1_.s2 = bf16[1088,1024]{1,0:T(8,128)(2,1)} collective-permute-done((bf16[1088,1024]{1,0:T(8,128)(2,1)}, bf16[1088,1024]{1,0:T(8,128)(2,1)}, u32[]{:S(2)}, u32[]{:S(2)}) %collective-permute-start.7) | collective-permute-done | bytes 2228256 | tf_op jit(solution)/shard_map/ppermute | solution.py:41
  65.9 2.6 %halves.2 = (bf16[512,1024]{1,0:T(8,128)(2,1)}, bf16[512,1024]{1,0:T(8,128)(2,1)}) custom-call(bf16[1088,1024]{1,0:T(8,128)(2,1)} %collective-permute-done.7.refs_0_.refs_1_.s2, bf16[1088,1024]{1,0:T(8,128)(2,1)} %copy-done.2), custom_call_target="tpu_custom_call" | custom-call | bytes 4000000 | tf_op jit(solution)/shard_map/halves/pallas_call | solution.py:62
  68.5 1.8 %gathered_priors.1.p0 = bf16[256,1024]{1,0:T(8,128)(2,1)} custom-call(bf16[64,1024]{1,0:T(8,128)(2,1)} %get-tuple-element.67.refs_0_, bf16[1088,1024]{1,0:T(8,128)(2,1)} %collective-permute-done.7.refs_0_.refs_1_.s2, bf16[1088,1024]{1,0:T(8,128)(2,1)} %copy-done.2, bf16[64,1024]{1,0:T(8,128)(2,1)} %copy-done.8), custom_call_target="tpu_custom_call" | custom-call | bytes 4000000 | tf_op jit(solution)/shard_map/gathered_priors/pallas_call | solution.py:62
  70.3 2.1 %collective-permute-start.17 = (bf16[256,1024]{1,0:T(8,128)(2,1)}, bf16[256,1024]{1,0:T(8,128)(2,1)S(1)}, u32[]{:S(2)}, u32[]{:S(2)}) collective-permute-start(bf16[256,1024]{1,0:T(8,128)(2,1)} %gathered_priors.1.p0), channel_id=1, source_target_pairs={{0,8},{8,0},{16,24},{24,16},{32,40},{40,32},{48,56},{56,48},{64,72... | collective-permute-start | bytes 1572872 | tf_op jit(solution)/shard_map/ppermute | solution.py:41
  72.4 1.2 %collective-permute-start.12 = (bf16[512,1024]{1,0:T(8,128)(2,1)}, bf16[512,1024]{1,0:T(8,128)(2,1)S(1)}, u32[]{:S(2)}, u32[]{:S(2)}) collective-permute-start(bf16[512,1024]{1,0:T(8,128)(2,1)} %get-tuple-element.85), channel_id=1, source_target_pairs={{0,64},{8,24},{16,80},{24,40},{32,96},{40,56},{48,112},{56,8},{64,... | collective-permute-start | bytes 3145736 | tf_op jit(solution)/shard_map/ppermute | solution.py:41
  73.6 1.5 %collective-permute-start.13 = (bf16[512,1024]{1,0:T(8,128)(2,1)}, bf16[512,1024]{1,0:T(8,128)(2,1)}, u32[]{:S(2)}, u32[]{:S(2)}) collective-permute-start(bf16[512,1024]{1,0:T(8,128)(2,1)} %get-tuple-element.86), channel_id=1, source_target_pairs={{0,192},{8,56},{16,208},{24,8},{32,224},{40,24},{48,240},{56,40},{... | collective-permute-start | bytes 3145736 | tf_op jit(solution)/shard_map/ppermute | solution.py:41
  75.8 6.4 %project.3 = (bf16[192,1024]{1,0:T(8,128)(2,1)}, bf16[192,384]{1,0:T(8,128)(2,1)}) custom-call(bf16[64,4096]{1,0:T(8,128)(2,1)} %copy-done.6, bf16[64,4096]{1,0:T(8,128)(2,1)} %copy-done.7, bf16[32,4096]{1,0:T(8,128)(2,1)} %copy-done.17, bf16[32,4096]{1,0:T(8,128)(2,1)} %copy-done.18, bf16[4096,1024]{1,0:T(8,128)(2,1)} %refs_4_, bf16[4096,256]{1,0:T(8,128)(2,1)} %bitcast.66, ...), custom_call_target="tpu_custom_call" | custom-call | flops 24000000000 | bytes 14000000 | tf_op jit(solution)/shard_map/project/pallas_call | solution.py:389
  83.9 13.8 %mixer_inner.1.refs_7_ = f32[10,544,128]{2,1,0:T(8,128)} custom-call(s32[1]{0:T(128)} %bitcast.12.where, s32[4,33]{1,0:T(4,128)} %pad.25.table.refs_0_, bf16[1088,1024]{1,0:T(8,128)(2,1)} %get-tuple-element.90.s0, bf16[1088,1024]{1,0:T(8,128)(2,1)} %collective-permute-done.16.s1, bf16[1088,1024]{1,0:T(8,128)(2,1)} %collective-permute-done.7.refs_0_.refs_1_.s2, ...), custom_call_target="tpu_custom_call" | custom-call | flops 14000000000 | bytes 18000000 | tf_op jit(solution)/shard_map/mixer_inner/pallas_call | solution.py:408
  97.7 1.6 %collective-permute-start.20 = (bf16[512,1024]{1,0:T(8,128)(2,1)S(1)}, bf16[512,1024]{1,0:T(8,128)(2,1)S(1)}, u32[]{:S(2)}, u32[]{:S(2)}) collective-permute-start(bf16[512,1024]{1,0:T(8,128)(2,1)S(1)} %collective-permute-done.12.refs_3_), channel_id=1, source_target_pairs={{0,8},{8,0},{16,24},{24,16},{32,40},{40,32},{48,56},{56,48},{64,72... | collective-permute-start | bytes 3145736 | tf_op jit(solution)/shard_map/ppermute | solution.py:41
  99.3 2.7 %collective-permute-done.20.refs_4_ = bf16[512,1024]{1,0:T(8,128)(2,1)S(1)} collective-permute-done((bf16[512,1024]{1,0:T(8,128)(2,1)S(1)}, bf16[512,1024]{1,0:T(8,128)(2,1)S(1)}, u32[]{:S(2)}, u32[]{:S(2)}) %collective-permute-start.20) | collective-permute-done | bytes 1048608 | tf_op jit(solution)/shard_map/ppermute | solution.py:41
  102.0 1.2 %collective-permute-done.21.refs_6_ = bf16[512,1024]{1,0:T(8,128)(2,1)S(1)} collective-permute-done((bf16[512,1024]{1,0:T(8,128)(2,1)}, bf16[512,1024]{1,0:T(8,128)(2,1)S(1)}, u32[]{:S(2)}, u32[]{:S(2)}) %collective-permute-start.21) | collective-permute-done | bytes 1048608 | tf_op jit(solution)/shard_map/ppermute | solution.py:41
  103.3 1.8 %copy-done = f32[10,544,128]{2,1,0:T(8,128)S(1)} copy-done((f32[10,544,128]{2,1,0:T(8,128)S(1)}, f32[10,544,128]{2,1,0:T(8,128)}, u32[]{:S(2)}) %copy-start) | copy-done | bytes 2785304
  105.0 5.9 %mixer_late.1 = bf16[512,1024]{1,0:T(8,128)(2,1)} custom-call(s32[4,33]{1,0:T(4,128)S(1)} %copy-done.1, bf16[1088,1024]{1,0:T(8,128)(2,1)S(1)} %collective-permute-done.18.refs_1_, bf16[1088,1024]{1,0:T(8,128)(2,1)} %collective-permute-done.19.refs_2_, bf16[512,1024]{1,0:T(8,128)(2,1)S(1)} %collective-permute-done.12.refs_3_, ...), custom_call_target="tpu_custom_call" | custom-call | flops 500000000 | bytes 13000000 | tf_op jit(solution)/shard_map/mixer_late/pallas_call | solution.py:434
  (87 shorter events, 12.7 us)
Async XLA Ops:
  0.0 13.8 %copy-start.12 = (s32[1,32]{1,0:T(1,128)S(1)}, s32[1,32]{1,0:T(1,128)}, u32[]{:S(2)}) copy-start(s32[1,32]{1,0:T(1,128)} %param.29) | copy-start | bytes 388
  0.0 13.9 %copy-start.10 = (bf16[4,2,128]{2,1,0:T(2,128)(2,1)S(1)}, bf16[4,2,128]{2,1,0:T(2,128)(2,1)}, u32[]{:S(2)}) copy-start(bf16[4,2,128]{2,1,0:T(2,128)(2,1)} %param.20) | copy-start | bytes 6148
  0.0 13.9 %copy-start.11 = (f32[16]{0:T(128)S(1)}, f32[16]{0:T(128)}, u32[]{:S(2)}) copy-start(f32[16]{0:T(128)} %param.23) | copy-start | bytes 196
  0.0 17.4 %copy-start.4 = (bf16[4096,2,128]{2,1,0:T(2,128)(2,1)S(1)}, bf16[4096,2,128]{2,1,0:T(2,128)(2,1)}, u32[]{:S(2)}) copy-start(bf16[4096,2,128]{2,1,0:T(2,128)(2,1)} %param.17) | copy-start | bytes 6291460
  0.0 19.7 %collective-permute-start.3 = (bf16[64,4096]{1,0:T(8,128)(2,1)}, bf16[64,4096]{1,0:T(8,128)(2,1)}, u32[]{:S(2)}, u32[]{:S(2)}) collective-permute-start(bf16[64,4096]{1,0:T(8,128)(2,1)} %refs_0_), channel_id=1, source_target_pairs={{0,1},{1,2},{2,3},{3,4},{4,5},{5,6},{6,7},{7,0},{8,9},{9,10},{10,1... | collective-permute-start | bytes 1572872 | tf_op jit(solution)/shard_map/ppermute | solution.py:37
  2.6 17.2 %collective-permute-start.5 = (bf16[64,4096]{1,0:T(8,128)(2,1)}, bf16[64,4096]{1,0:T(8,128)(2,1)}, u32[]{:S(2)}, u32[]{:S(2)}) collective-permute-start(bf16[64,4096]{1,0:T(8,128)(2,1)} %refs_0_), channel_id=1, source_target_pairs={{0,7},{1,0},{2,1},{3,2},{4,3},{5,4},{6,5},{7,6},{8,15},{9,8},{10,9... | collective-permute-start | bytes 1572872 | tf_op jit(solution)/shard_map/ppermute | solution.py:37
  9.3 9.8 %copy-start.3 = (bf16[272,1024]{1,0:T(8,128)(2,1)}, bf16[272,1024]{1,0:T(8,128)(2,1)S(1)}, u32[]{:S(2)}) copy-start(bf16[272,1024]{1,0:T(8,128)(2,1)S(1)} %fusion.1.refs_0_) | copy-start | bytes 1671172
  9.3 14.9 %collective-permute-start.2 = (bf16[272,1024]{1,0:T(8,128)(2,1)S(1)}, bf16[272,1024]{1,0:T(8,128)(2,1)S(1)}, u32[]{:S(2)}, u32[]{:S(2)}) collective-permute-start(bf16[272,1024]{1,0:T(8,128)(2,1)S(1)} %fusion.1.refs_0_), channel_id=1, source_target_pairs={{0,32},{8,136},{16,48},{24,152},{32,0},{40,168},{48,16},{56,184},{... | collective-permute-start | bytes 1671176 | tf_op jit(solution)/shard_map/ppermute | solution.py:41
  12.3 13.7 %collective-permute-start.1 = (bf16[272,1024]{1,0:T(8,128)(2,1)S(1)}, bf16[272,1024]{1,0:T(8,128)(2,1)}, u32[]{:S(2)}, u32[]{:S(2)}) collective-permute-start(bf16[272,1024]{1,0:T(8,128)(2,1)S(1)} %fusion.1.refs_0_), channel_id=1, source_target_pairs={{0,48},{8,200},{16,0},{24,216},{32,16},{40,232},{48,32},{56,248},{... | collective-permute-start | bytes 1671176 | tf_op jit(solution)/shard_map/ppermute | solution.py:41
  13.1 13.0 %collective-permute-start = (bf16[272,1024]{1,0:T(8,128)(2,1)S(1)}, bf16[272,1024]{1,0:T(8,128)(2,1)}, u32[]{:S(2)}, u32[]{:S(2)}) collective-permute-start(bf16[272,1024]{1,0:T(8,128)(2,1)S(1)} %fusion.1.refs_0_), channel_id=1, source_target_pairs={{0,16},{8,72},{16,32},{24,88},{32,48},{40,104},{48,0},{56,120},{64... | collective-permute-start | bytes 1671176 | tf_op jit(solution)/shard_map/ppermute | solution.py:41
  17.4 5.6 %copy-start.14 = (f32[16]{0:T(128)S(1)}, f32[16]{0:T(128)}, u32[]{:S(2)}) copy-start(f32[16]{0:T(128)} %param.21) | copy-start | bytes 196
  17.4 6.2 %copy-start.9 = (bf16[4,1024]{1,0:T(4,128)(2,1)S(1)}, bf16[4,1024]{1,0:T(4,128)(2,1)}, u32[]{:S(2)}) copy-start(bf16[4,1024]{1,0:T(4,128)(2,1)} %param.19) | copy-start | bytes 24580
  19.7 13.4 %collective-permute-start.4 = (bf16[64,4096]{1,0:T(8,128)(2,1)}, bf16[64,4096]{1,0:T(8,128)(2,1)}, u32[]{:S(2)}, u32[]{:S(2)}) collective-permute-start(bf16[64,4096]{1,0:T(8,128)(2,1)} %collective-permute-done.3.refs_1_), channel_id=1, source_target_pairs={{0,1},{1,2},{2,3},{3,4},{4,5},{5,6},{6,7},{7,0},{8,9},{9,10},{10,1... | collective-permute-start | bytes 1572872 | tf_op jit(solution)/shard_map/ppermute | solution.py:37
  19.8 13.3 %collective-permute-start.6 = (bf16[64,4096]{1,0:T(8,128)(2,1)}, bf16[64,4096]{1,0:T(8,128)(2,1)S(1)}, u32[]{:S(2)}, u32[]{:S(2)}) collective-permute-start(bf16[64,4096]{1,0:T(8,128)(2,1)} %collective-permute-done.5.refs_2_), channel_id=1, source_target_pairs={{0,7},{1,0},{2,1},{3,2},{4,3},{5,4},{6,5},{7,6},{8,15},{9,8},{10,9... | collective-permute-start | bytes 1572872 | tf_op jit(solution)/shard_map/ppermute | solution.py:37
  33.1 6.0 %copy-start.15 = (bf16[64,4096]{1,0:T(8,128)(2,1)}, bf16[64,4096]{1,0:T(8,128)(2,1)S(1)}, u32[]{:S(2)}) copy-start(bf16[64,4096]{1,0:T(8,128)(2,1)S(1)} %collective-permute-done.6.refs_4_) | copy-start | bytes 1572868
  33.1 8.7 %collective-permute-start.9 = (bf16[64,1024]{1,0:T(8,128)(2,1)}, bf16[64,1024]{1,0:T(8,128)(2,1)S(1)}, u32[]{:S(2)}, u32[]{:S(2)}) collective-permute-start(bf16[64,1024]{1,0:T(8,128)(2,1)} %get-tuple-element.67.refs_0_), channel_id=1, source_target_pairs={{0,128},{8,40},{16,144},{24,56},{32,160},{40,8},{48,176},{56,24},{... | collective-permute-start | bytes 393224 | tf_op jit(solution)/shard_map/ppermute | solution.py:41
  37.6 26.9 %collective-permute-start.8 = (bf16[1088,1024]{1,0:T(8,128)(2,1)}, bf16[1088,1024]{1,0:T(8,128)(2,1)S(1)}, u32[]{:S(2)}, u32[]{:S(2)}) collective-permute-start(bf16[1088,1024]{1,0:T(8,128)(2,1)} %get-tuple-element.90.s0), channel_id=1, source_target_pairs={{0,192},{8,56},{16,208},{24,8},{32,224},{40,24},{48,240},{56,40},{... | collective-permute-start | bytes 6684680 | tf_op jit(solution)/shard_map/ppermute | solution.py:41
  37.7 28.1 %collective-permute-start.7 = (bf16[1088,1024]{1,0:T(8,128)(2,1)}, bf16[1088,1024]{1,0:T(8,128)(2,1)}, u32[]{:S(2)}, u32[]{:S(2)}) collective-permute-start(bf16[1088,1024]{1,0:T(8,128)(2,1)} %get-tuple-element.90.s0), channel_id=1, source_target_pairs={{0,64},{8,24},{16,80},{24,40},{32,96},{40,56},{48,112},{56,8},{64,... | collective-permute-start | bytes 6684680 | tf_op jit(solution)/shard_map/ppermute | solution.py:41
  39.1 14.6 %collective-permute-start.10 = (bf16[64,4096]{1,0:T(8,128)(2,1)}, bf16[64,4096]{1,0:T(8,128)(2,1)S(1)}, u32[]{:S(2)}, u32[]{:S(2)}) collective-permute-start(bf16[64,4096]{1,0:T(8,128)(2,1)} %collective-permute-done.4.refs_3_), channel_id=1, source_target_pairs={{0,1},{1,2},{2,3},{3,4},{4,5},{5,6},{6,7},{7,0},{8,9},{9,10},{10,1... | collective-permute-start | bytes 1572872 | tf_op jit(solution)/shard_map/ppermute | solution.py:37
  39.1 14.6 %collective-permute-start.11 = (bf16[64,4096]{1,0:T(8,128)(2,1)}, bf16[64,4096]{1,0:T(8,128)(2,1)S(1)}, u32[]{:S(2)}, u32[]{:S(2)}) collective-permute-start(bf16[64,4096]{1,0:T(8,128)(2,1)} %copy-done.15), channel_id=1, source_target_pairs={{0,7},{1,0},{2,1},{3,2},{4,3},{5,4},{6,5},{7,6},{8,15},{9,8},{10,9... | collective-permute-start | bytes 1572872 | tf_op jit(solution)/shard_map/ppermute | solution.py:37
  41.8 8.9 %copy-start.8 = (bf16[64,1024]{1,0:T(8,128)(2,1)}, bf16[64,1024]{1,0:T(8,128)(2,1)S(1)}, u32[]{:S(2)}) copy-start(bf16[64,1024]{1,0:T(8,128)(2,1)S(1)} %collective-permute-done.9.refs_3_) | copy-start | bytes 393220
  41.8 33.3 %collective-permute-start.16 = (bf16[1088,1024]{1,0:T(8,128)(2,1)}, bf16[1088,1024]{1,0:T(8,128)(2,1)}, u32[]{:S(2)}, u32[]{:S(2)}) collective-permute-start(bf16[1088,1024]{1,0:T(8,128)(2,1)} %get-tuple-element.90.s0), channel_id=1, source_target_pairs={{0,8},{8,0},{16,24},{24,16},{32,40},{40,32},{48,56},{56,48},{64,72... | collective-permute-start | bytes 6684680 | tf_op jit(solution)/shard_map/ppermute | solution.py:41
  56.5 17.1 %collective-permute-start.14 = (bf16[32,4096]{1,0:T(8,128)(2,1)}, bf16[32,4096]{1,0:T(8,128)(2,1)S(1)}, u32[]{:S(2)}, u32[]{:S(2)}) collective-permute-start(bf16[32,4096]{1,0:T(8,128)(2,1)} %get-tuple-element.88), channel_id=1, source_target_pairs={{0,1},{1,2},{2,3},{3,4},{4,5},{5,6},{6,7},{7,0},{8,9},{9,10},{10,1... | collective-permute-start | bytes 786440 | tf_op jit(solution)/shard_map/ppermute | solution.py:37
  57.8 17.4 %collective-permute-start.15 = (bf16[32,4096]{1,0:T(8,128)(2,1)}, bf16[32,4096]{1,0:T(8,128)(2,1)S(1)}, u32[]{:S(2)}, u32[]{:S(2)}) collective-permute-start(bf16[32,4096]{1,0:T(8,128)(2,1)} %get-tuple-element.89), channel_id=1, source_target_pairs={{0,7},{1,0},{2,1},{3,2},{4,3},{5,4},{6,5},{7,6},{8,15},{9,8},{10,9... | collective-permute-start | bytes 786440 | tf_op jit(solution)/shard_map/ppermute | solution.py:37
  70.3 12.8 %collective-permute-start.17 = (bf16[256,1024]{1,0:T(8,128)(2,1)}, bf16[256,1024]{1,0:T(8,128)(2,1)S(1)}, u32[]{:S(2)}, u32[]{:S(2)}) collective-permute-start(bf16[256,1024]{1,0:T(8,128)(2,1)} %gathered_priors.1.p0), channel_id=1, source_target_pairs={{0,8},{8,0},{16,24},{24,16},{32,40},{40,32},{48,56},{56,48},{64,72... | collective-permute-start | bytes 1572872 | tf_op jit(solution)/shard_map/ppermute | solution.py:41
  72.4 25.2 %collective-permute-start.12 = (bf16[512,1024]{1,0:T(8,128)(2,1)}, bf16[512,1024]{1,0:T(8,128)(2,1)S(1)}, u32[]{:S(2)}, u32[]{:S(2)}) collective-permute-start(bf16[512,1024]{1,0:T(8,128)(2,1)} %get-tuple-element.85), channel_id=1, source_target_pairs={{0,64},{8,24},{16,80},{24,40},{32,96},{40,56},{48,112},{56,8},{64,... | collective-permute-start | bytes 3145736 | tf_op jit(solution)/shard_map/ppermute | solution.py:41
  73.6 24.0 %collective-permute-start.13 = (bf16[512,1024]{1,0:T(8,128)(2,1)}, bf16[512,1024]{1,0:T(8,128)(2,1)}, u32[]{:S(2)}, u32[]{:S(2)}) collective-permute-start(bf16[512,1024]{1,0:T(8,128)(2,1)} %get-tuple-element.86), channel_id=1, source_target_pairs={{0,192},{8,56},{16,208},{24,8},{32,224},{40,24},{48,240},{56,40},{... | collective-permute-start | bytes 3145736 | tf_op jit(solution)/shard_map/ppermute | solution.py:41
  82.2 21.0 %collective-permute-start.18 = (bf16[1088,1024]{1,0:T(8,128)(2,1)}, bf16[1088,1024]{1,0:T(8,128)(2,1)S(1)}, u32[]{:S(2)}, u32[]{:S(2)}) collective-permute-start(bf16[1088,1024]{1,0:T(8,128)(2,1)} %collective-permute-done.7.refs_0_.refs_1_.s2), channel_id=1, source_target_pairs={{0,8},{8,0},{16,24},{24,16},{32,40},{40,32},{48,56},{56,48},{64,72... | collective-permute-start | bytes 6684680 | tf_op jit(solution)/shard_map/ppermute | solution.py:41
  83.0 20.3 %collective-permute-start.19 = (bf16[1088,1024]{1,0:T(8,128)(2,1)}, bf16[1088,1024]{1,0:T(8,128)(2,1)}, u32[]{:S(2)}, u32[]{:S(2)}) collective-permute-start(bf16[1088,1024]{1,0:T(8,128)(2,1)} %copy-done.2), channel_id=1, source_target_pairs={{0,8},{8,0},{16,24},{24,16},{32,40},{40,32},{48,56},{56,48},{64,72... | collective-permute-start | bytes 6684680 | tf_op jit(solution)/shard_map/ppermute | solution.py:41
  83.9 19.4 %copy-start.1 = (s32[4,33]{1,0:T(4,128)S(1)}, s32[4,33]{1,0:T(4,128)}, u32[]{:S(2)}) copy-start(s32[4,33]{1,0:T(4,128)} %pad.25.table.refs_0_) | copy-start | bytes 1588
  97.7 4.3 %collective-permute-start.20 = (bf16[512,1024]{1,0:T(8,128)(2,1)S(1)}, bf16[512,1024]{1,0:T(8,128)(2,1)S(1)}, u32[]{:S(2)}, u32[]{:S(2)}) collective-permute-start(bf16[512,1024]{1,0:T(8,128)(2,1)S(1)} %collective-permute-done.12.refs_3_), channel_id=1, source_target_pairs={{0,8},{8,0},{16,24},{24,16},{32,40},{40,32},{48,56},{56,48},{64,72... | collective-permute-start | bytes 3145736 | tf_op jit(solution)/shard_map/ppermute | solution.py:41
  99.2 4.0 %collective-permute-start.21 = (bf16[512,1024]{1,0:T(8,128)(2,1)}, bf16[512,1024]{1,0:T(8,128)(2,1)S(1)}, u32[]{:S(2)}, u32[]{:S(2)}) collective-permute-start(bf16[512,1024]{1,0:T(8,128)(2,1)} %collective-permute-done.13.refs_5_), channel_id=1, source_target_pairs={{0,8},{8,0},{16,24},{24,16},{32,40},{40,32},{48,56},{56,48},{64,72... | collective-permute-start | bytes 3145736 | tf_op jit(solution)/shard_map/ppermute | solution.py:41
  (9 other events, 15.4 us)
